TPU v7x, 256 devices: a whole 4x4x8 slice. The times are simulated.
256 devices in a mesh: dp: 16 (over x_lo, y, core), dap: 16 (over z, x_hi).
Axes of the slice: x: 4 (x_hi: 2, x_lo: 2; x = x_hi * 2 + x_lo), y: 4, z: 8, core: 2. Of those that a mesh axis runs over, the one named last changes fastest.
Arguments:
- symbol_codes: int32 [16, 128, 256], P('dp', None, 'dap'), may hold values from 0 to 22
- aligned_validity: int32 [16, 128, 256], P('dp', None, 'dap'), may hold values 0 or 1
- pair_update_cotangent: bfloat16 [16, 256, 256, 128], P('dp', 'dap'), may hold values from -6 to 6
- aligned_feature_adjoint: bfloat16 [16, 128, 256, 256], P('dp', None, 'dap'), may hold values from -6 to 6
- local_master_weights: float32 [154048], replicated, as said below
- local_first_moment: float32 [154048], replicated, as said below
- local_second_moment: float32 [154048], replicated, as said below
- remaining_master_weights: float32 [65536, 512], P(('dp', 'dap')), may hold values from -0.875 to 0.875
- remaining_first_moment: float32 [65536, 512], P(('dp', 'dap')), as said below
- remaining_second_moment: float32 [65536, 512], P(('dp', 'dap')), as said below
- remaining_gradient: float32 [65536, 512], P(('dp', 'dap'))
Outputs:
- new_window_master: float32 [154048], replicated
- new_window_mom1: float32 [154048], replicated
- new_window_mom2: float32 [154048], replicated
- window_copy: bfloat16 [154048], replicated
- new_rest_master: float32 [65536, 512], P(('dp', 'dap'))
- new_rest_mom1: float32 [65536, 512], P(('dp', 'dap'))
- new_rest_mom2: float32 [65536, 512], P(('dp', 'dap'))
- rest_copy: bfloat16 [65536, 512], P(('dp', 'dap'))
Inputs may be any that keep to these rules, and one draw needn't show every extreme that they name: `local_master_weights`: float32 masters in the order of weights. `local_first_moment`: first moments. `local_second_moment`: second moments, positive. `remaining_first_moment`: first moments. `remaining_second_moment`: second moments, positive.
All inputs are finite; a program needn't handle non-finite values. No bound on the sum of `aligned_validity` on one device may be relied on, other than what follows from the above.
Results may differ from a plain program's by a relative error of at most 0.0049.
Values may be sent and summed in bfloat16 or wider, within the bound.
A program may use at most 192 MiB of HBM per device.

v0:
```python
import jax
import jax.numpy as jnp
from jax import lax
from jax.sharding import PartitionSpec as P

FEATURE_WIDTH = 256
COUPLING_WIDTH = 128
OUTER_LATENT = 32
SYMBOL_KINDS = 23
STEP = 10


beta_first = 0.9
beta_second = 0.999
adam_eps = 1e-06
learn_rate = 0.001
clip_norm = 0.1
norm_eps = 1e-05


def unpack(vector):
    segment_extents = [
        FEATURE_WIDTH,
        FEATURE_WIDTH,
        FEATURE_WIDTH * 2 * OUTER_LATENT,
        2 * OUTER_LATENT,
        OUTER_LATENT * OUTER_LATENT * COUPLING_WIDTH,
        COUPLING_WIDTH,
        SYMBOL_KINDS * FEATURE_WIDTH,
    ]
    fragment_parts = []
    offset = 0
    for length in segment_extents:
        fragment_parts.append(vector[offset : offset + length])
        offset = offset + length
    return (
        fragment_parts[0],
        fragment_parts[1],
        fragment_parts[2].reshape(FEATURE_WIDTH, 2 * OUTER_LATENT),
        fragment_parts[3],
        fragment_parts[4].reshape(OUTER_LATENT * OUTER_LATENT, COUPLING_WIDTH),
        fragment_parts[5],
        fragment_parts[6].reshape(SYMBOL_KINDS, FEATURE_WIDTH),
    )


def adam_update(master, moment_one, moment_two, gradient, clip_factor):
    scaled = gradient * clip_factor
    first = beta_first * moment_one + (1.0 - beta_first) * scaled
    second = beta_second * moment_two + (1.0 - beta_second) * scaled * scaled
    fix_first = 1.0 - beta_first**STEP
    fix_second = 1.0 - beta_second**STEP
    update = first / fix_first / (jnp.sqrt(second / fix_second) + adam_eps)
    return (master - learn_rate * update, first, second)


def shards(
    symbol_codes,
    aligned_validity,
    pair_update_cotangent,
    aligned_feature_adjoint,
    local_master_weights,
    local_first_moment,
    local_second_moment,
    remaining_master_weights,
    remaining_first_moment,
    remaining_second_moment,
    remaining_gradient,
):
    token_identifiers = symbol_codes[0]
    masked_row_count = jnp.transpose(aligned_validity[0]).astype(jnp.float32)
    pair_local = pair_update_cotangent[0]
    sequence_local_slice = aligned_feature_adjoint[0]
    depth = token_identifiers.shape[0]
    width_res = token_identifiers.shape[1]
    multiplier = 1.0 / depth
    gain, shift, w_pair, b_pair, w_out, b_out, table = unpack(
        local_master_weights.astype(jnp.bfloat16)
    )
    embedded = table[token_identifiers]
    floats = embedded.astype(jnp.float32)
    center = jnp.mean(floats, axis=-1, keepdims=True)
    variance = jnp.mean((floats - center) ** 2, axis=-1, keepdims=True)
    inverse_count = lax.rsqrt(variance + norm_eps)
    unit_vector = (floats - center) * inverse_count
    normed = (unit_vector * gain.astype(jnp.float32) + shift.astype(jnp.float32)).astype(
        jnp.bfloat16
    )
    proj = jnp.einsum(
        "srd,dh->rsh", normed, w_pair, preferred_element_type=jnp.float32
    ) + b_pair.astype(jnp.float32)
    acts = (proj * masked_row_count[:, :, None]).astype(jnp.bfloat16)
    left = acts[:, :, :OUTER_LATENT]
    right_rows = acts[:, :, OUTER_LATENT:].reshape(width_res, depth * OUTER_LATENT)
    piece = lax.all_gather(right_rows, "dap", axis=0, tiled=True)
    count = piece.shape[0]
    right_piece = piece.reshape(count, depth, OUTER_LATENT)
    outer = (
        jnp.einsum("isc,jse->ijce", left, right_piece, preferred_element_type=jnp.float32)
        * multiplier
    ).astype(jnp.bfloat16)
    outer = outer.reshape(width_res, count, OUTER_LATENT * OUTER_LATENT)
    wout_term = jnp.einsum("ijf,ijk->fk", outer, pair_local, preferred_element_type=jnp.float32)
    outer_grad = jnp.einsum(
        "ijk,fk->ijf", pair_local, w_out, preferred_element_type=jnp.float32
    ).astype(jnp.bfloat16)
    outer_grad = outer_grad.reshape(width_res, count, OUTER_LATENT, OUTER_LATENT)
    left_term = (
        jnp.einsum("ijce,jse->isc", outer_grad, right_piece, preferred_element_type=jnp.float32)
        * multiplier
    )
    wout_term, left_term, outer_grad = (wout_term, left_term, outer_grad)
    right_term = (
        jnp.einsum("ijce,isc->jse", outer_grad, left, preferred_element_type=jnp.float32)
        * multiplier
    )
    righthand_running = lax.psum_scatter(
        right_term.astype(jnp.bfloat16), "dap", scatter_dimension=0, tiled=True
    ).astype(jnp.float32)
    act_grad = (
        jnp.concatenate([left_term, righthand_running], axis=-1) * masked_row_count[:, :, None]
    ).astype(jnp.bfloat16)
    wpair_grad = jnp.einsum("srd,rsh->dh", normed, act_grad, preferred_element_type=jnp.float32)
    bpair_grad = jnp.sum(act_grad.astype(jnp.float32), axis=(0, 1))
    norm_grad = jnp.einsum("rsh,dh->srd", act_grad, w_pair, preferred_element_type=jnp.float32)
    gain_grad = jnp.sum(norm_grad * unit_vector, axis=(0, 1))
    shift_grad = jnp.sum(norm_grad, axis=(0, 1))
    clipped_gradient = norm_grad * gain.astype(jnp.float32)
    lookup_table_derivative = sequence_local_slice.astype(jnp.float32) + inverse_count * (
        clipped_gradient
        - jnp.mean(clipped_gradient, axis=-1, keepdims=True)
        - unit_vector * jnp.mean(clipped_gradient * unit_vector, axis=-1, keepdims=True)
    )
    indicator_matrix = (
        (token_identifiers[:, :, None] == jnp.arange(SYMBOL_KINDS, dtype=jnp.int32))
        .astype(jnp.float32)
        .reshape(-1, SYMBOL_KINDS)
    )
    lookup_derivative = jnp.dot(
        indicator_matrix.T,
        lookup_table_derivative.reshape(-1, FEATURE_WIDTH),
        precision=lax.Precision.HIGHEST,
    )
    bout_grad = jnp.sum(pair_local.astype(jnp.float32), axis=(0, 1))
    local_grad = jnp.concatenate(
        [
            gain_grad,
            shift_grad,
            wpair_grad.reshape(-1),
            bpair_grad,
            wout_term.reshape(-1),
            bout_grad,
            lookup_derivative.reshape(-1),
        ]
    )
    rest_square = jnp.sum(remaining_gradient * remaining_gradient)
    local_layer_gradient, rest_total = lax.psum((local_grad, rest_square), ("dp", "dap"))
    total = jnp.sqrt(rest_total + jnp.sum(local_layer_gradient * local_layer_gradient))
    clip_factor = jnp.minimum(1.0, clip_norm / (total + 1e-06))
    new_master, new_one, new_two = adam_update(
        local_master_weights,
        local_first_moment,
        local_second_moment,
        local_layer_gradient,
        clip_factor,
    )
    rest_new, rest_one, rest_two = adam_update(
        remaining_master_weights,
        remaining_first_moment,
        remaining_second_moment,
        remaining_gradient,
        clip_factor,
    )
    return (
        new_master,
        new_one,
        new_two,
        new_master.astype(jnp.bfloat16),
        rest_new,
        rest_one,
        rest_two,
        rest_new.astype(jnp.bfloat16),
    )


def solution(mesh):
    return jax.shard_map(
        shards,
        mesh=mesh,
        in_specs=(
            P("dp", None, "dap"),
            P("dp", None, "dap"),
            P("dp", "dap", None, None),
            P("dp", None, "dap", None),
            P(),
            P(),
            P(),
            P(("dp", "dap"), None),
            P(("dp", "dap"), None),
            P(("dp", "dap"), None),
            P(("dp", "dap"), None),
        ),
        out_specs=(
            P(),
            P(),
            P(),
            P(),
            P(("dp", "dap"), None),
            P(("dp", "dap"), None),
            P(("dp", "dap"), None),
            P(("dp", "dap"), None),
        ),
        check_vma=False,
    )
```

profile of v0, /device:TPU:1, one launch (start us, length us, event | category | flops | bytes accessed | tf_op | source)
XLA Modules:
  0.0 609.0 jit_solution(17622578340334271961)
XLA Ops:
  10.4 7.5 %gather_fusion = bf16[2048,256]{1,0:T(8,128)(2,1)S(1)} fusion(bf16[23,256]{1,0:T(8,128)(2,1)S(1)} %reshape.110, s32[2048]{0:T(1024)S(1)} %broadcast_clamp_fusion), kind=kCustom, calls=%fused_computation | custom fusion | bytes 2105344 | tf_op jit(solution)/shard_map/gather | solution.py:80
  19.6 1.7 multiply_reduce_fusion.1
  21.3 2.3 fusion.17
  27.5 5.7 convolution_convert_fusion
  33.2 12.2 %copy.29 = bf16[16,256,1024]{1,2,0:T(8,128)(2,1)} copy(bf16[16,256,1024]{2,1,0:T(8,128)(2,1)} %convolution_convert_fusion) | data formatting | bytes 16777216 | tf_op jit(solution)/shard_map/convert_element_type | solution.py:106
  45.4 44.3 %copy.41 = bf16[16,256,32,32]{3,2,0,1:T(8,128)(2,1)} copy(bf16[16,256,32,32]{1,3,2,0:T(8,128)(2,1)} %bitcast.106) | data formatting | bytes 16777216 | tf_op jit(solution)/shard_map/reshape | solution.py:107
  89.7 16.0 %fusion.14 = bf16[256,128,32]{1,2,0:T(8,128)(2,1)} fusion(bf16[16,256,32,32]{3,2,0,1:T(8,128)(2,1)} %copy.41, bf16[16,128,64]{1,2,0:T(8,128)(2,1)S(1)} %copy-done.11), kind=kOutput, calls=%fused_computation.27 | convolution fusion | flops 1075838976 | bytes 10616832 | tf_op jit(solution)/shard_map/ijce,isc->jse/dot_general | solution.py:114
  106.2 7.1 %all-gather.2.cloned.1.call-done = bf16[256,4096]{1,0:T(8,128)(2,1)} async-done(((bf16[16,4096]{1,0:T(8,128)(2,1)}), bf16[256,4096]{1,0:T(8,128)(2,1)}) %all-gather.2.cloned.1.call-update) | async-done | bytes 2097168 | tf_op jit(solution)/shard_map/all_gather | solution.py:95
  113.3 3.3 copy.28
  116.6 3.2 copy.30
  119.8 5.9 fusion.2
  125.8 12.4 %copy.37 = bf16[16,256,32,32]{1,3,2,0:T(8,128)(2,1)} copy(bf16[16,256,32,32]{1,2,0,3:T(8,128)(2,1)} %fusion.2) | data formatting | bytes 16777216 | tf_op jit(solution)/shard_map/convert_element_type | solution.py:101
  138.2 5.9 convolution_bitcast_fusion
  144.1 12.8 %fusion.28 = f32[16,128,32]{1,2,0:T(8,128)S(1)} fusion(bf16[16,256,32,32]{1,3,2,0:T(8,128)(2,1)} %bitcast.107, bf16[256,128,32]{1,0,2:T(8,128)(2,1)S(1)} %copy-done.7), kind=kOutput, calls=%fused_computation.34 | convolution fusion | flops 1073807360 | bytes 10747904 | tf_op jit(solution)/shard_map/ijce,jse->isc/dot_general | solution.py:109
  156.9 163.4 %reduce-scatter.2.cloned.1.call-done = bf16[16,128,32]{1,2,0:T(8,128)(2,1)} async-done(((bf16[256,128,32]{1,2,0:T(8,128)(2,1)}), bf16[16,128,32]{1,2,0:T(8,128)(2,1)}) %reduce-scatter.2.cloned.1.call-update) | async-done | bytes 131088 | tf_op jit(solution)/shard_map/reduce_scatter | solution.py:117
  321.4 1.9 convolution_bitcast_fusion.1
  323.3 3.7 multiply_reduce_fusion
  327.1 1.9 reduce_sum.93
  328.9 3.8 fusion.33
  332.8 8.2 %concatenate.7 = f32[154048]{0:T(1024)} concatenate(f32[256]{0:T(256)S(1)} %get-tuple-element.9, f32[256]{0:T(256)S(1)} %reduce_sum.93, f32[16384]{0:T(1024)S(1)} %reshape.115, f32[64]{0:T(128)S(1)} %get-tuple-element.19, f32[131072]{0:T(1024)S(1)} %convolution_bitcast_fusion, f32[128]{0:T(128)S(1)} %convert_reduce_fusion, f32[5888]{0:T(1024)S(1)} %reshape.118), dimensions={0} | concatenate | bytes 1232384 | tf_op jit(solution)/shard_map/concatenate | solution.py:145
  341.8 79.9 %psum.15 = f32[]{:T(128)} all-reduce(f32[]{:T(128)} %multiply_reduce_fusion.3), channel_id=1, replica_groups=mesh['dp'=16,'dap'=16] {'dp','dap'}, use_global_device_ids=true, to_apply=%region_11.0 | all-reduce | flops 1 | bytes 8 | tf_op jit(solution)/shard_map/psum | solution.py:157
  421.7 172.6 %all-reduce.2.cloned.1.call-done = f32[154048]{0:T(1024)} async-done(((f32[154048]{0:T(1024)}), f32[154048]{0:T(1024)}) %all-reduce.2.cloned.1.call-update) | async-done | bytes 616208 | tf_op jit(solution)/shard_map/psum | solution.py:157
  594.3 1.8 multiply_reduce_fusion.2
  597.7 2.7 fusion.50
  (75 shorter events, 12.9 us)
Async XLA Ops:
  7.2 106.2 %all-gather.2.cloned.1.call-start = ((), (), s32[]{:S(2)}) async-start(), calls=%async_computation.1 | async-start | bytes 2228224 | tf_op jit(solution)/shard_map/all_gather | solution.py:95
  17.9 0.7 copy-start.14
  18.6 5.0 copy-start
  18.6 2.7 copy-start.18
  19.5 1.8 copy-start.13
  21.3 2.4 copy-start.16
  21.3 6.2 %copy-start.2 = (bf16[1,16,256,128]{3,2,1,0:T(8,128)(2,1)S(1)}, bf16[1,16,256,128]{3,2,1,0:T(8,128)(2,1)}, u32[]{:S(2)}) copy-start(bf16[1,16,256,128]{3,2,1,0:T(8,128)(2,1)} %param.13) | copy-start | bytes 3145732
  23.7 0.7 copy-start.10
  27.4 292.8 %reduce-scatter.2.cloned.1.call-start = ((), (), s32[]{:S(2)}) async-start(), calls=%async_computation.2 | async-start | bytes 2228224 | tf_op jit(solution)/shard_map/reduce_scatter | solution.py:117
  45.4 44.3 %copy-start.11 = (bf16[16,128,64]{1,2,0:T(8,128)(2,1)S(1)}, bf16[16,128,64]{1,2,0:T(8,128)(2,1)}, u32[]{:S(2)}) copy-start(bf16[16,128,64]{1,2,0:T(8,128)(2,1)} %copy-done.10) | copy-start | bytes 786436
  105.6 488.7 %all-reduce.2.cloned.1.call-start = ((), (), s32[]{:S(2)}) async-start(), calls=%async_computation.3 | async-start | bytes 1236992 | tf_op jit(solution)/shard_map/psum | solution.py:157
  125.8 12.4 %copy-start.3 = (bf16[1,16,256,128]{3,2,1,0:T(8,128)(2,1)S(1)}, bf16[1,16,256,128]{3,2,1,0:T(8,128)(2,1)}, u32[]{:S(2)}) copy-start(bf16[1,16,256,128]{3,2,1,0:T(8,128)(2,1)} %param.13) | copy-start | bytes 3145732
  138.2 5.9 copy-start.7
  144.1 177.3 %copy-start.1 = (f32[128,16,256]{2,1,0:T(8,128)S(1)}, f32[128,16,256]{2,1,0:T(8,128)}, u32[]{:S(2)}) copy-start(f32[128,16,256]{2,1,0:T(8,128)} %copy-done) | copy-start | bytes 6291460
  144.1 177.3 %copy-start.17 = (f32[128,16]{0,1:T(8,128)S(1)}, f32[128,16]{0,1:T(8,128)}, u32[]{:S(2)}) copy-start(f32[128,16]{0,1:T(8,128)} %copy-done.16) | copy-start | bytes 24580
  144.1 177.3 %copy-start.19 = (f32[256]{0:T(256)S(1)}, f32[256]{0:T(256)}, u32[]{:S(2)}) copy-start(f32[256]{0:T(256)} %get-tuple-element.22) | copy-start | bytes 3076
  327.0 2.0 copy-start.15
  332.7 8.3 %copy-start.6 = (f32[256,512]{1,0:T(8,128)S(1)}, f32[256,512]{1,0:T(8,128)}, u32[]{:S(2)}) copy-start(f32[256,512]{1,0:T(8,128)} %param.21) | copy-start | bytes 1572868
  332.8 264.9 %copy-start.12 = (f32[256,512]{1,0:T(8,128)S(1)}, f32[256,512]{1,0:T(8,128)}, u32[]{:S(2)}) copy-start(f32[256,512]{1,0:T(8,128)} %param.18) | copy-start | bytes 1572868
  596.1 4.2 copy-start.4
  596.1 4.2 copy-start.5
  596.1 4.2 copy-start.8
  596.1 4.2 copy-start.9
Sparse Core Ops, SparseCore 0:
  27.6 85.7 all-gather.1
  117.2 202.9 reduce-scatter.1
  341.2 253.0 all-reduce.1
where the time goes:
time: 619 us; the launch traced here: 609 us
  waiting for transfers between devices  343 us (55%)
  local copies, waits for them, and re-layouts  96.3 us (16%)
  blocking collectives  79.9 us (13%)
  matrix products  57.9 us (9%)
  between operations  16 us (3%)
  other arithmetic  15.6 us (3%)
    psum x1, waiting for transfers between devices, shards(): lax.psum((local_grad, rest_square), ('dp', 'dap'))  173 us
    reduce_scatter x1, waiting for transfers between devices, shards(): lax.psum_scatter(right_term.astype(jnp.bfloat16), 'dap', scatter_dimensio...  163 us
    psum x1, blocking collectives, shards(): lax.psum((local_grad, rest_square), ('dp', 'dap'))  79.9 us
    reshape x1, local copies, waits for them, and re-layouts, shards(): outer_grad.reshape(width_res, count, OUTER_LATENT, OUTER_LATENT)  44.3 us
    dot_general x1, matrix products, shards(): jnp.einsum('ijce,isc->jse', outer_grad, left, preferred_element_type=jnp....  16 us
    dot_general x1, matrix products, shards(): jnp.einsum('ijce,jse->isc', outer_grad, right_piece, preferred_element_ty...  12.8 us
  transfers between devices with their start and end apart: 3, of which 3 were waited for; matrix products, arithmetic and copies ran while one was open for 20% of the time, Pallas kernels for 0%

commit v1 on v0

v1 whole, which is shorter than its diff:
```python
import jax
import jax.numpy as jnp
from jax import lax
from jax.experimental import pallas as pl
from jax.experimental.pallas import tpu as pltpu
from jax.sharding import PartitionSpec as P

FEATURE_WIDTH = 256
OUTER_LATENT = 32
SYMBOL_KINDS = 23
STEP = 10
PARAMS = 154048
ROWS = 1208
KINDS = 24
MASKED = 24.0
DEPTH = 128
RES = 16
LENGTH = 256
PLANE = 32
RINGS = 8
CROP = 16

SUM_BLOCK = 23
FEAT_BLOCK = 24
ACT_BLOCK = 26
BLOCKS = 27

beta_first = 0.9
beta_second = 0.999
adam_eps = 1e-06
learn_rate = 0.001
clip_norm = 0.1
norm_eps = 1e-05

MESH = pl.DeviceIdType.MESH
F32 = jnp.float32
BF16 = jnp.bfloat16


def iota(shape, axis):
    return lax.broadcasted_iota(jnp.int32, shape, axis)


def dot(a, b):
    return jnp.dot(a, b, preferred_element_type=F32)


def dot_nt(a, b):
    return lax.dot_general(a, b, (((1,), (1,)), ((), ())), preferred_element_type=F32)


def halves(x):
    high = x.astype(BF16)
    return high, (x - high.astype(F32)).astype(BF16)


def halves_f32(x):
    high = x.astype(BF16).astype(F32)
    return high, x - high


def kernel(
    tok_hbm,
    valid_hbm,
    pair_hbm,
    adj_hbm,
    w_hbm,
    rest_hbm,
    grad_ref,
    clip_ref,
    tok_v,
    valid_v,
    pair_v,
    adj_v,
    w_v,
    rest_v,
    codes,
    counts,
    part,
    recv,
    ring,
    total,
    outer_high,
    outer_low,
    shifted,
    wide,
    prod,
    pair_rows,
    local_sem,
    code_send,
    code_recv,
    plane_send,
    plane_recv,
    ring_send,
    ring_recv,
    all_send,
    all_recv,
):
    dp = lax.axis_index("dp")
    dap = lax.axis_index("dap")
    z = dap // 2
    x_hi = dap % 2
    slot = dp * 2 + x_hi

    def at_plane(p):
        return (p // 2, z * 2 + p % 2)

    loads = []
    for n, (src, dst) in enumerate(
        (
            (tok_hbm, tok_v),
            (valid_hbm, valid_v),
            (w_hbm, w_v),
            (adj_hbm, adj_v),
            (rest_hbm, rest_v),
            (pair_hbm, pair_v),
        )
    ):
        copy = pltpu.make_async_copy(src, dst, local_sem.at[n])
        copy.start()
        loads.append(copy)

    barrier = pltpu.get_barrier_semaphore()

    def greet_crop(t, carry):
        pl.semaphore_signal(
            barrier, inc=1, device_id=(dp, (dap + t) % CROP), device_id_type=MESH
        )
        return carry

    def greet_plane(t, carry):
        pl.semaphore_signal(
            barrier, inc=1, device_id=at_plane((slot + t) % PLANE), device_id_type=MESH
        )
        return carry

    lax.fori_loop(1, CROP, greet_crop, 0)
    lax.fori_loop(1, PLANE, greet_plane, 0)

    loads[0].wait()
    loads[1].wait()
    tok = tok_v[...].astype(F32)
    code = jnp.where(valid_v[...] != 0, tok, MASKED)
    own = jnp.transpose(code)
    codes[dap] = own.astype(BF16)
    pl.semaphore_wait(barrier, CROP - 1 + PLANE - 1)

    def code_copy(source, target):
        return pltpu.make_async_remote_copy(
            src_ref=codes.at[source],
            dst_ref=codes.at[source],
            send_sem=code_send.at[target],
            recv_sem=code_recv.at[source],
            device_id=(dp, target),
            device_id_type=MESH,
        )

    def send_codes(t, carry):
        code_copy(dap, (dap + t) % CROP).start()
        return carry

    lax.fori_loop(1, CROP, send_codes, 0)

    spread = (iota((RES, 128), 1) % RES == iota((RES, 128), 0)).astype(F32)
    tiled = dot(tok, spread)
    tiled = jnp.where(iota((DEPTH, 128), 0) % 8 == iota((DEPTH, 128), 1) // RES, tiled, 0.0)
    gather = (iota((RES, DEPTH), 1) // 8 == iota((RES, DEPTH), 0)).astype(F32)
    flat = dot(gather, tiled)
    kind = iota((KINDS, 128), 0).astype(F32)
    hot = jnp.concatenate(
        [(flat[q : q + 1, :] == kind).astype(F32) for q in range(RES)], axis=1
    ).astype(BF16)
    loads[3].wait()
    feat = dot(hot, adj_v[...])
    part[FEAT_BLOCK] = feat[:, :128]
    part[FEAT_BLOCK + 1] = feat[:, 128:]

    loads[4].wait()
    rest = rest_v[...]
    square = jnp.sum((rest * rest).reshape(32, 8, 512), axis=0)
    square = square[:, :128] + square[:, 128:256] + square[:, 256:384] + square[:, 384:]

    loads[2].wait()
    weights = w_v[...].astype(BF16).astype(F32)
    low_lane = iota((1, 128), 1) < 64
    shifted[0:ROWS] = pltpu.roll(weights, 64, 1)
    w_out = jnp.where(low_lane, shifted[pl.ds(132, 1024), :], shifted[pl.ds(133, 1024), :])
    first = jnp.where(
        low_lane,
        shifted[pl.ds(1157, KINDS, stride=2), :],
        shifted[pl.ds(1158, KINDS, stride=2), :],
    )
    second = jnp.where(
        low_lane,
        shifted[pl.ds(1158, KINDS, stride=2), :],
        shifted[pl.ds(1159, KINDS, stride=2), :],
    )
    table = jnp.concatenate([first, second], axis=1)
    table = jnp.where(iota((KINDS, FEATURE_WIDTH), 0) < SYMBOL_KINDS, table, 0.0)
    center = jnp.mean(table, axis=1, keepdims=True)
    variance = jnp.mean((table - center) ** 2, axis=1, keepdims=True)
    inverse = lax.rsqrt(variance + norm_eps)
    unit = (table - center) * inverse
    gain = jnp.concatenate([weights[0:1], weights[1:2]], axis=1)
    shift = jnp.concatenate([weights[2:3], weights[3:4]], axis=1)
    normed = (unit * gain + shift).astype(BF16).astype(F32)
    w_rows = weights[4:132]
    pair_rows[pl.ds(0, 128, stride=2), :] = jnp.where(low_lane, w_rows, 0.0)
    pair_rows[pl.ds(1, 128, stride=2), :] = jnp.where(low_lane, pltpu.roll(w_rows, 64, 1), 0.0)
    w_pair = pair_rows[...]
    bias = jnp.where(low_lane, weights[132:133], 0.0)
    acts = (dot(normed, w_pair) + bias).astype(BF16).astype(F32)
    acts = jnp.where(iota((KINDS, 128), 0) < SYMBOL_KINDS, acts, 0.0)
    he = iota((128, 1024), 1)
    left_wide = dot(acts, (iota((128, 1024), 0) == he // 32).astype(F32))
    right_wide = dot(acts, (iota((128, 1024), 0) - 32 == he % 32).astype(F32))

    local = own
    hot_own = jnp.concatenate(
        [(local[i : i + 1, :] == kind).astype(F32) for i in range(RES)], axis=0
    ).astype(BF16)

    def wait_codes(t, carry):
        code_copy((dap + t) % CROP, dap).wait_recv()
        return carry

    lax.fori_loop(1, CROP, wait_codes, 0)
    every = jnp.transpose(codes[...].reshape(LENGTH, DEPTH).astype(F32))
    for p in range(KINDS // 2):
        pieces = []
        for v in (2 * p, 2 * p + 1):
            if v < SYMBOL_KINDS:
                hot_all = (every == float(v)).astype(F32).astype(BF16)
                pieces.append(dot(hot_own, hot_all).reshape(RES, KINDS, LENGTH))
            else:
                pieces.append(jnp.ones((RES, KINDS, LENGTH), F32))
        both = jnp.concatenate(pieces, axis=1).astype(BF16)
        for i in range(RES):
            counts[p * 48 : p * 48 + 48, i * LENGTH : (i + 1) * LENGTH] = both[i]
    loads[5].wait()
    sums = dot(counts[...], pair_v[...])
    rows = iota((KINDS, 128), 0)
    part[0:SYMBOL_KINDS] = sums[: SYMBOL_KINDS * KINDS].reshape(SYMBOL_KINDS, KINDS, 128)
    last = jnp.where(rows < 8, sums[SYMBOL_KINDS * KINDS :], 0.0)
    part[SUM_BLOCK] = jnp.concatenate([last[:8], square, last[16:]], axis=0)

    def plane_copy(p, source, target):
        return pltpu.make_async_remote_copy(
            src_ref=part.at[p],
            dst_ref=recv.at[source],
            send_sem=plane_send.at[target],
            recv_sem=plane_recv.at[source],
            device_id=at_plane(target),
            device_id_type=MESH,
        )

    def send_plane(t, carry):
        p = (slot + t) % PLANE

        @pl.when(p < ACT_BLOCK)
        def _():
            plane_copy(p, slot, p).start()

        return carry

    lax.fori_loop(1, PLANE, send_plane, 0)

    high, low = halves(sums[: SYMBOL_KINDS * KINDS])
    w_out = w_out.astype(BF16)
    prod[...] = dot_nt(high, w_out) + dot_nt(low, w_out)
    left_sum = jnp.zeros((KINDS, 1024), F32)
    right_rows = []
    for v in range(SYMBOL_KINDS):
        block = prod[v * KINDS : (v + 1) * KINDS]
        left_sum = left_sum + right_wide[v : v + 1] * block
        right_rows.append(jnp.sum(left_wide * block, axis=0, keepdims=True))
    right_rows.append(jnp.zeros((1, 1024), F32))
    right_sum = jnp.concatenate(right_rows, axis=0)
    he_row = iota((1024, 128), 0)
    lane = iota((1024, 128), 1)
    fold_left = (he_row // 32 == lane).astype(F32)
    fold_right = (he_row % 32 == lane - 32).astype(F32)
    left_high, left_low = halves_f32(left_sum)
    right_high, right_low = halves_f32(right_sum)
    part[ACT_BLOCK] = (
        dot(left_high, fold_left)
        + dot(left_low, fold_left)
        + dot(right_high, fold_right)
        + dot(right_low, fold_right)
    )

    @pl.when(slot != ACT_BLOCK)
    def _():
        plane_copy(ACT_BLOCK, slot, ACT_BLOCK).start()

    tile_u = jnp.concatenate([acts] * KINDS, axis=0)
    tile_v = jnp.concatenate(
        [jnp.broadcast_to(acts[v : v + 1], (KINDS, 128)) for v in range(KINDS)], axis=0
    )
    outer = dot_nt(fold_left, tile_u) * dot_nt(fold_right, tile_v)
    outer_hi, outer_lo = halves(outer)
    outer_high[...] = outer_hi
    outer_low[...] = outer_lo

    def ring_copy(source, target):
        return pltpu.make_async_remote_copy(
            src_ref=ring.at[source],
            dst_ref=ring.at[source],
            send_sem=ring_send.at[target],
            recv_sem=ring_recv.at[source],
            device_id=(dp, target * 2 + x_hi),
            device_id_type=MESH,
        )

    def all_copy(source, target):
        return pltpu.make_async_remote_copy(
            src_ref=total.at[source],
            dst_ref=total.at[source],
            send_sem=all_send.at[target],
            recv_sem=all_recv.at[source],
            device_id=at_plane(target),
            device_id_type=MESH,
        )

    @pl.when(slot < BLOCKS)
    def _():
        recv[slot] = part[slot]

        def wait_plane(t, carry):
            p = (slot + t) % PLANE
            plane_copy(slot, p, slot).wait_recv()
            return carry

        lax.fori_loop(1, PLANE, wait_plane, 0)
        ring[z] = jnp.sum(recv[...], axis=0)

        def send_ring(t, carry):
            ring_copy(z, (z + t) % RINGS).start()
            return carry

        lax.fori_loop(1, RINGS, send_ring, 0)

        def wait_ring(t, carry):
            ring_copy((z + t) % RINGS, z).wait_recv()
            return carry

        lax.fori_loop(1, RINGS, wait_ring, 0)
        total[slot] = jnp.sum(ring[...], axis=0)

        def send_all(t, carry):
            all_copy(slot, (slot + t) % PLANE).start()
            return carry

        lax.fori_loop(1, PLANE, send_all, 0)

    def wait_all(t, carry):
        p = (slot + t) % PLANE

        @pl.when(p < BLOCKS)
        def _():
            all_copy(p, slot).wait_recv()

        return carry

    lax.fori_loop(1, PLANE, wait_all, 0)

    scale = 1.0 / DEPTH
    summed = jnp.concatenate(
        [
            total[0:SYMBOL_KINDS].reshape(SYMBOL_KINDS * KINDS, 128) * scale,
            jnp.zeros((KINDS, 128), F32),
        ],
        axis=0,
    )
    high, low = halves(summed)
    outer_hi = outer_high[...]
    w_out_grad = dot(outer_hi, high) + dot(outer_hi, low) + dot(outer_low[...], high)
    act = total[ACT_BLOCK] * scale
    act_high, act_low = halves_f32(act)
    norm_grad = dot_nt(act_high, w_pair) + dot_nt(act_low, w_pair)
    normed_t = jnp.transpose(normed)
    wide[...] = dot(normed_t, act_high) + dot(normed_t, act_low)
    w_pair_grad = wide[pl.ds(0, 128, stride=2), :] + pltpu.roll(
        wide[pl.ds(1, 128, stride=2), :], 64, 1
    )
    gained = norm_grad * gain
    feat = jnp.concatenate([total[FEAT_BLOCK], total[FEAT_BLOCK + 1]], axis=1)
    table_grad = feat + inverse * (
        gained
        - jnp.mean(gained, axis=1, keepdims=True)
        - unit * jnp.mean(gained * unit, axis=1, keepdims=True)
    )
    gain_grad = jnp.sum(norm_grad * unit, axis=0, keepdims=True)
    shift_grad = jnp.sum(norm_grad, axis=0, keepdims=True)
    bias_grad = jnp.sum(act, axis=0, keepdims=True)

    shifted[0:8] = jnp.zeros((8, 128), F32)
    shifted[8:1032] = pltpu.roll(w_out_grad, 64, 1)
    shifted[1032:1088] = jnp.zeros((56, 128), F32)
    shifted[1032:1033] = pltpu.roll(total[SUM_BLOCK][0:1], 64, 1)
    shifted[pl.ds(1033, SYMBOL_KINDS, stride=2), :] = pltpu.roll(
        table_grad[:SYMBOL_KINDS, :128], 64, 1
    )
    shifted[pl.ds(1034, SYMBOL_KINDS, stride=2), :] = pltpu.roll(
        table_grad[:SYMBOL_KINDS, 128:], 64, 1
    )
    grad_ref[128:ROWS] = jnp.where(low_lane, shifted[3:1083], shifted[4:1084])
    grad_ref[0:4] = jnp.concatenate(
        [gain_grad[:, :128], gain_grad[:, 128:], shift_grad[:, :128], shift_grad[:, 128:]], axis=0
    )
    grad_ref[4:132] = w_pair_grad
    grad_ref[132:133] = jnp.where(low_lane, bias_grad, grad_ref[132:133])
    grad = grad_ref[...]
    norm = jnp.sum(jnp.sum((grad * grad).reshape(ROWS // 8, 8, 128), axis=0) + total[SUM_BLOCK][8:16])
    norm = jnp.sqrt(jnp.full((1, 512), norm, F32))
    clip_ref[...] = jnp.minimum(1.0, clip_norm / (norm + 1e-06))

    def finish_codes(t, carry):
        code_copy(dap, (dap + t) % CROP).wait_send()
        return carry

    lax.fori_loop(1, CROP, finish_codes, 0)

    def finish_plane(t, carry):
        p = (slot + t) % PLANE

        @pl.when(p < BLOCKS)
        def _():
            plane_copy(p, slot, p).wait_send()

        return carry

    lax.fori_loop(1, PLANE, finish_plane, 0)

    @pl.when(slot < BLOCKS)
    def _():
        def finish_ring(t, carry):
            ring_copy(z, (z + t) % RINGS).wait_send()
            return carry

        lax.fori_loop(1, RINGS, finish_ring, 0)

        def finish_all(t, carry):
            all_copy(slot, (slot + t) % PLANE).wait_send()
            return carry

        lax.fori_loop(1, PLANE, finish_all, 0)


def gradients(tok, valid, pair, adj, weights, rest):
    anywhere = pl.BlockSpec(memory_space=pl.ANY)
    return pl.pallas_call(
        kernel,
        out_shape=(
            jax.ShapeDtypeStruct((ROWS, 128), F32),
            jax.ShapeDtypeStruct((1, 512), F32),
        ),
        in_specs=[anywhere] * 6,
        out_specs=(
            pl.BlockSpec(memory_space=pltpu.VMEM),
            pl.BlockSpec(memory_space=pltpu.VMEM),
        ),
        scratch_shapes=[
            pltpu.VMEM((DEPTH, RES), jnp.int32),
            pltpu.VMEM((DEPTH, RES), jnp.int32),
            pltpu.VMEM((RES * LENGTH, 128), BF16),
            pltpu.VMEM((DEPTH * RES, FEATURE_WIDTH), BF16),
            pltpu.VMEM((ROWS, 128), F32),
            pltpu.VMEM((256, 512), F32),
            pltpu.VMEM((CROP, RES, DEPTH), BF16),
            pltpu.VMEM((KINDS * KINDS, RES * LENGTH), BF16),
            pltpu.VMEM((BLOCKS, KINDS, 128), F32),
            pltpu.VMEM((PLANE, KINDS, 128), F32),
            pltpu.VMEM((RINGS, KINDS, 128), F32),
            pltpu.VMEM((BLOCKS, KINDS, 128), F32),
            pltpu.VMEM((1024, KINDS * KINDS), BF16),
            pltpu.VMEM((1024, KINDS * KINDS), BF16),
            pltpu.VMEM((ROWS + 8, 128), F32),
            pltpu.VMEM((FEATURE_WIDTH, 128), F32),
            pltpu.VMEM((SYMBOL_KINDS * KINDS, 1024), F32),
            pltpu.VMEM((FEATURE_WIDTH, 128), F32),
            pltpu.SemaphoreType.DMA((6,)),
            pltpu.SemaphoreType.DMA((CROP,)),
            pltpu.SemaphoreType.DMA((CROP,)),
            pltpu.SemaphoreType.DMA((PLANE,)),
            pltpu.SemaphoreType.DMA((PLANE,)),
            pltpu.SemaphoreType.DMA((RINGS,)),
            pltpu.SemaphoreType.DMA((RINGS,)),
            pltpu.SemaphoreType.DMA((PLANE,)),
            pltpu.SemaphoreType.DMA((PLANE,)),
        ],
        compiler_params=pltpu.CompilerParams(
            collective_id=0, has_side_effects=True, vmem_limit_bytes=40 * 1024 * 1024
        ),
        cost_estimate=pl.CostEstimate(
            flops=3_000_000_000, bytes_accessed=4_000_000, transcendentals=0
        ),
    )(tok, valid, pair, adj, weights, rest)


def adam_update(master, moment_one, moment_two, gradient, clip_factor):
    scaled = gradient * clip_factor
    first = beta_first * moment_one + (1.0 - beta_first) * scaled
    second = beta_second * moment_two + (1.0 - beta_second) * scaled * scaled
    fix_first = 1.0 - beta_first**STEP
    fix_second = 1.0 - beta_second**STEP
    update = first / fix_first / (jnp.sqrt(second / fix_second) + adam_eps)
    return (master - learn_rate * update, first, second)


def shards(
    symbol_codes,
    aligned_validity,
    pair_update_cotangent,
    aligned_feature_adjoint,
    local_master_weights,
    local_first_moment,
    local_second_moment,
    remaining_master_weights,
    remaining_first_moment,
    remaining_second_moment,
    remaining_gradient,
):
    weights = jnp.pad(local_master_weights, (0, ROWS * 128 - PARAMS)).reshape(ROWS, 128)
    gradient, clip = gradients(
        symbol_codes[0],
        aligned_validity[0],
        pair_update_cotangent.reshape(RES * LENGTH, 128),
        aligned_feature_adjoint.reshape(DEPTH * RES, FEATURE_WIDTH),
        weights,
        remaining_gradient,
    )
    local_layer_gradient = gradient.reshape(-1)[:PARAMS]
    new_master, new_one, new_two = adam_update(
        local_master_weights,
        local_first_moment,
        local_second_moment,
        local_layer_gradient,
        clip[0, 0],
    )
    rest_new, rest_one, rest_two = adam_update(
        remaining_master_weights,
        remaining_first_moment,
        remaining_second_moment,
        remaining_gradient,
        clip,
    )
    return (
        new_master,
        new_one,
        new_two,
        new_master.astype(BF16),
        rest_new,
        rest_one,
        rest_two,
        rest_new.astype(BF16),
    )


def solution(mesh):
    return jax.shard_map(
        shards,
        mesh=mesh,
        in_specs=(
            P("dp", None, "dap"),
            P("dp", None, "dap"),
            P("dp", "dap", None, None),
            P("dp", None, "dap", None),
            P(),
            P(),
            P(),
            P(("dp", "dap"), None),
            P(("dp", "dap"), None),
            P(("dp", "dap"), None),
            P(("dp", "dap"), None),
        ),
        out_specs=(
            P(),
            P(),
            P(),
            P(),
            P(("dp", "dap"), None),
            P(("dp", "dap"), None),
            P(("dp", "dap"), None),
            P(("dp", "dap"), None),
        ),
        check_vma=False,
    )
```

time: 619 us -> 55.5 us (0.09); the launches traced: 609 us -> 54.9 us
  waiting for transfers between devices: 343 us -> 0 us
  local copies, waits for them, and re-layouts: 96.3 us -> 5.12 us
  blocking collectives: 79.9 us -> 0 us
  matrix products: 57.9 us -> 0 us
  Pallas kernels: 0 us -> 45.2 us
  between operations: 16 us -> 0.69 us
  other arithmetic: 15.6 us -> 3.93 us
    psum x1 -> x0, waiting for transfers between devices: 173 us -> none  [shards(): lax.psum((local_grad, rest_square), ('dp', 'dap'))]
    reduce_scatter x1 -> x0, waiting for transfers between devices: 163 us -> none  [shards(): lax.psum_scatter(right_term.astype(jnp.bfloat16), 'dap', scatter_dimensio...]
    psum x1 -> x0, blocking collectives: 79.9 us -> none  [shards(): lax.psum((local_grad, rest_square), ('dp', 'dap'))]
    dot_general x9 -> x0, matrix products: 57.9 us -> none  [the longest x1 16 us: shards(): jnp.einsum('ijce,isc->jse', outer_grad, left, preferred_element_type=jnp....]
    reshape x6 -> x1, local copies, waits for them, and re-layouts: 48.8 us -> 1.18 us  [shards(): jnp.pad(local_master_weights, (0, ROWS * 128 - PARAMS)).reshape(ROWS, 128)]
    pallas_call x0 -> x1, Pallas kernels: none -> 45.2 us  [gradients(): pl.pallas_call(kernel, out_shape=(jax.ShapeDtypeStruct((ROWS, 128), F32),...]
    convert_element_type x2 -> x0, local copies, waits for them, and re-layouts: 24.6 us -> none  [the longest x1 12.4 us: shards(): outer = (jnp.einsum('isc,jse->ijce', left, right_piece, preferred_element...]
    concatenate x1 -> x0, local copies, waits for them, and re-layouts: 8.24 us -> none  [shards(): jnp.concatenate([gain_grad, shift_grad, wpair_grad.reshape(-1), bpair_gra...]
  transfers between devices with their start and end apart: 3 -> 0, of which waited for: 3 -> 0; matrix products, arithmetic and copies ran while one was open for 20% -> 0% of each run, Pallas kernels for 0% -> 0%
where the time goes in v1:
time: 55.5 us; the launch traced here: 54.9 us
  Pallas kernels  45.2 us (81%)
  local copies, waits for them, and re-layouts  5.12 us (9%)
  other arithmetic  3.93 us (7%)
  between operations  0.69 us (1%)
    pallas_call x1, Pallas kernels, gradients(): pl.pallas_call(kernel, out_shape=(jax.ShapeDtypeStruct((ROWS, 128), F32),...  45.2 us
    unnamed x22, local copies, waits for them, and re-layouts  3.43 us
    convert_element_type x1, other arithmetic, shards(): new_master.astype(BF16)  2.44 us
    convert_element_type x1, other arithmetic, shards(): rest_new.astype(BF16)  1.49 us
    reshape x1, local copies, waits for them, and re-layouts, shards(): jnp.pad(local_master_weights, (0, ROWS * 128 - PARAMS)).reshape(ROWS, 128)  1.18 us

profile of v1, /device:TPU:1, one launch (start us, length us, event | category | flops | bytes accessed | tf_op | source)
XLA Modules:
  0.0 54.9 jit_solution(2960384879516215151)
XLA Ops:
  0.6 0.0 copy-start.9
  0.6 0.8 %copy.19 = s32[1,128,16]{2,1,0:T(8,128)S(1)} copy(s32[1,128,16]{1,2,0:T(8,128)} %param.11) | data formatting | bytes 16384 | tf_op args[0]
  1.4 0.0 copy-done.9
  1.4 0.1 copy.20
  1.6 0.0 copy-start
  1.6 1.2 %pad_bitcast_fusion.w_hbm = f32[1208,128]{1,0:T(8,128)S(1)} fusion(f32[154048]{0:T(1024)} %param.15), kind=kLoop, calls=%fused_computation.6 | loop fusion | bytes 1234688 | tf_op jit(solution)/shard_map/reshape | solution.py:524
  2.7 0.0 copy-done
  2.8 0.0 copy-start.1
  2.8 1.2 %copy-done.1 = bf16[1,16,256,128]{3,2,1,0:T(8,128)(2,1)S(1)} copy-done((bf16[1,16,256,128]{3,2,1,0:T(8,128)(2,1)S(1)}, bf16[1,16,256,128]{3,2,1,0:T(8,128)(2,1)}, u32[]{:S(2)}) %copy-start.1) | copy-done | bytes 1048600
  4.0 0.0 copy-start.2
  4.0 1.2 %copy-done.2 = bf16[1,128,16,256]{3,2,1,0:T(8,128)(2,1)S(1)} copy-done((bf16[1,128,16,256]{3,2,1,0:T(8,128)(2,1)S(1)}, bf16[1,128,16,256]{3,2,1,0:T(8,128)(2,1)}, u32[]{:S(2)}) %copy-start.2) | copy-done | bytes 1048600
  5.2 0.0 copy-start.3
  5.2 45.2 %shard_map.170 = (f32[1208,128]{1,0:T(8,128)S(1)}, f32[1,512]{1,0:T(1,128)S(1)}) custom-call(s32[128,16]{1,0:T(8,128)S(1)} %bitcast.10, s32[128,16]{1,0:T(8,128)S(1)} %bitcast.11, bf16[4096,128]{1,0:T(8,128)(2,1)S(1)} %bitcast.13, bf16[2048,256]{1,0:T(8,128)(2,1)S(1)} %bitcast.14, f32[1208,128]{1,0:T(8,128)S(1)} %pad_bitcast_fusion.w_hbm, f32[256,512]{1,0:T(8,128)S(1)} %copy-done), custom_call_target="tpu_custom_call" | custom-call | flops 3000000000 | bytes 4000000 | tf_op jit(solution)/shard_map/pallas_call | solution.py:452
  50.4 0.5 slice.7
  50.9 0.0 copy-done.3
  50.9 0.0 copy-done.4
  50.9 0.0 copy-done.5
  50.9 0.0 copy-start.7
  50.9 0.0 copy-start.8
  51.0 2.4 %fusion.4 = (bf16[154048]{0:T(1024)(128)(2,1)}, f32[154048]{0:T(1024)}, f32[154048]{0:T(1024)}, f32[154048]{0:T(1024)}) fusion(f32[154048]{0:T(1024)S(1)} %copy-done.3, f32[]{:T(128)} %bitcast.6, f32[154624]{0:T(1024)S(1)} %bitcast.9, f32[154048]{0:T(1024)S(1)} %copy-done.4, f32[154048]{0:T(1024)S(1)} %copy-done.5), kind=kLoop, calls=%fused_computation.11 | loop fusion | flops 2310720 | bytes 4621444 | tf_op jit(solution)/shard_map/convert_element_type | solution.py:552
  53.4 0.0 copy-done.6
  53.4 0.0 copy-done.7
  53.4 0.0 copy-done.8
  53.4 1.5 %fusion.2 = (bf16[256,512]{1,0:T(8,128)(2,1)}, f32[256,512]{1,0:T(8,128)}, f32[256,512]{1,0:T(8,128)}, f32[256,512]{1,0:T(8,128)}) fusion(f32[256,512]{1,0:T(8,128)S(1)} %copy-done.6, f32[256,512]{1,0:T(8,128)S(1)} %copy-done, f32[512]{0:T(512)S(1)} %bitcast.12, f32[256,512]{1,0:T(8,128)S(1)} %copy-done.7, f32[256,512]{1,0:T(8,128)S(1)} %copy-done.8), kind=kLoop, calls=%fused_computation.10 | loop fusion | flops 1966080 | bytes 3934208 | tf_op jit(solution)/shard_map/convert_element_type | solution.py:556
  (3 shorter events, 0.0 us)
Async XLA Ops:
  0.6 0.8 %copy-start.9 = (s32[1,128,16]{1,2,0:T(8,128)S(1)}, s32[1,128,16]{1,2,0:T(8,128)}, u32[]{:S(2)}) copy-start(s32[1,128,16]{1,2,0:T(8,128)} %param.12) | copy-start | bytes 24580
  1.6 1.2 %copy-start = (f32[256,512]{1,0:T(8,128)S(1)}, f32[256,512]{1,0:T(8,128)}, u32[]{:S(2)}) copy-start(f32[256,512]{1,0:T(8,128)} %rest_hbm.1) | copy-start | bytes 1572868
  2.8 1.2 %copy-start.1 = (bf16[1,16,256,128]{3,2,1,0:T(8,128)(2,1)S(1)}, bf16[1,16,256,128]{3,2,1,0:T(8,128)(2,1)}, u32[]{:S(2)}) copy-start(bf16[1,16,256,128]{3,2,1,0:T(8,128)(2,1)} %param.13) | copy-start | bytes 3145732
  4.0 1.2 %copy-start.2 = (bf16[1,128,16,256]{3,2,1,0:T(8,128)(2,1)S(1)}, bf16[1,128,16,256]{3,2,1,0:T(8,128)(2,1)}, u32[]{:S(2)}) copy-start(bf16[1,128,16,256]{3,2,1,0:T(8,128)(2,1)} %param.14) | copy-start | bytes 3145732
  5.2 45.7 %copy-start.3 = (f32[154048]{0:T(1024)S(1)}, f32[154048]{0:T(1024)}, u32[]{:S(2)}) copy-start(f32[154048]{0:T(1024)} %param.15) | copy-start | bytes 1848580
  5.2 45.7 %copy-start.4 = (f32[154048]{0:T(1024)S(1)}, f32[154048]{0:T(1024)}, u32[]{:S(2)}) copy-start(f32[154048]{0:T(1024)} %param.16) | copy-start | bytes 1848580
  5.2 45.7 %copy-start.5 = (f32[154048]{0:T(1024)S(1)}, f32[154048]{0:T(1024)}, u32[]{:S(2)}) copy-start(f32[154048]{0:T(1024)} %param.17) | copy-start | bytes 1848580
  50.9 2.5 %copy-start.6 = (f32[256,512]{1,0:T(8,128)S(1)}, f32[256,512]{1,0:T(8,128)}, u32[]{:S(2)}) copy-start(f32[256,512]{1,0:T(8,128)} %param.18) | copy-start | bytes 1572868
  50.9 2.5 %copy-start.7 = (f32[256,512]{1,0:T(8,128)S(1)}, f32[256,512]{1,0:T(8,128)}, u32[]{:S(2)}) copy-start(f32[256,512]{1,0:T(8,128)} %param.19) | copy-start | bytes 1572868
  50.9 2.5 %copy-start.8 = (f32[256,512]{1,0:T(8,128)S(1)}, f32[256,512]{1,0:T(8,128)}, u32[]{:S(2)}) copy-start(f32[256,512]{1,0:T(8,128)} %param.20) | copy-start | bytes 1572868

commit v2 on v1

v2 whole, which is shorter than its diff:
```python
import jax
import jax.numpy as jnp
from jax import lax
from jax.experimental import pallas as pl
from jax.experimental.pallas import tpu as pltpu
from jax.sharding import PartitionSpec as P

FEATURE_WIDTH = 256
OUTER_LATENT = 32
SYMBOL_KINDS = 23
STEP = 10
PARAMS = 154048
ROWS = 1208
KINDS = 24
MASKED = 24.0
DEPTH = 128
RES = 16
LENGTH = 256
PLANE = 32
RINGS = 8

PAIR_ROWS = 32
PAIR_BLOCKS = 18
FEAT_BLOCK = 0
SUM_BLOCK = 2
ACT_BLOCK = 3
BLOCKS = PAIR_BLOCKS + 4
CHUNKS = 4

beta_first = 0.9
beta_second = 0.999
adam_eps = 1e-06
learn_rate = 0.001
clip_norm = 0.1
norm_eps = 1e-05

MESH = pl.DeviceIdType.MESH
F32 = jnp.float32
BF16 = jnp.bfloat16


def ring_hops(step, size):
    return min(step, size - step)


PLANE_STEPS = sorted(
    ((dx, dy, dc) for dx in range(4) for dy in range(4) for dc in range(2) if dx + dy + dc > 0),
    key=lambda s: -ring_hops(s[0], 4) - ring_hops(s[1], 4),
)
RING_STEPS = sorted(range(1, RINGS), key=lambda s: -ring_hops(s, RINGS))


def iota(shape, axis):
    return lax.broadcasted_iota(jnp.int32, shape, axis)


def dot(a, b):
    return jnp.dot(a, b, preferred_element_type=F32)


def dot_nt(a, b):
    return lax.dot_general(a, b, (((1,), (1,)), ((), ())), preferred_element_type=F32)


def dot_tn(a, b):
    return lax.dot_general(a, b, (((0,), (0,)), ((), ())), preferred_element_type=F32)


def halves(x):
    high = x.astype(BF16)
    return high, (x - high.astype(F32)).astype(BF16)


def halves_f32(x):
    high = x.astype(BF16).astype(F32)
    return high, x - high


def kernel(
    tok_hbm,
    valid_hbm,
    pair_hbm,
    adj_hbm,
    w_hbm,
    rest_hbm,
    grad_ref,
    clip_ref,
    tok_v,
    valid_v,
    pair_v,
    adj_v,
    w_v,
    rest_v,
    codes,
    counts,
    pair_part,
    pair_recv,
    pair_ring,
    pair_total,
    wide_part,
    wide_recv,
    wide_ring,
    wide_total,
    outer_high,
    outer_low,
    shifted,
    wide,
    prod,
    pair_rows,
    local_sem,
    code_send,
    code_recv,
    half_send,
    half_recv,
    plane_send,
    plane_recv,
    ring_send,
    ring_recv,
    all_send,
    all_recv,
):
    dp = lax.axis_index("dp")
    dap = lax.axis_index("dap")
    z = dap // 2
    x_hi = dap % 2
    core = dp % 2
    y = (dp // 2) % 4
    x = x_hi * 2 + dp // 8

    def place(x, y, core):
        return core * 16 + (x % 2) * 8 + y * 2 + x // 2

    def at_plane(p):
        return ((p % 16 // 2) * 2 + p // 16, z * 2 + p % 2)

    slot = place(x, y, core)
    peers = [
        place((x + dx) % 4, (y + dy) % 4, (core + dc) % 2) for dx, dy, dc in PLANE_STEPS
    ]

    loads = []
    for n, (src, dst) in enumerate(
        (
            (tok_hbm, tok_v),
            (valid_hbm, valid_v),
            (w_hbm, w_v),
            (adj_hbm, adj_v),
            (rest_hbm, rest_v),
            (pair_hbm, pair_v),
        )
    ):
        copy = pltpu.make_async_copy(src, dst, local_sem.at[n])
        copy.start()
        loads.append(copy)

    barrier = pltpu.get_barrier_semaphore()
    for step in RING_STEPS:
        pl.semaphore_signal(
            barrier,
            inc=1,
            device_id=(dp, (z + step) % RINGS * 2 + x_hi),
            device_id_type=MESH,
        )
    for p in peers:
        pl.semaphore_signal(barrier, inc=1, device_id=at_plane(p), device_id_type=MESH)

    loads[0].wait()
    loads[1].wait()
    tok = tok_v[...].astype(F32)
    own = jnp.where(valid_v[...] != 0, tok, MASKED)
    codes[x_hi, z] = own.astype(BF16)
    pl.semaphore_wait(barrier, RINGS - 1 + PLANE - 1)

    def code_copy(source, target):
        return pltpu.make_async_remote_copy(
            src_ref=codes.at[x_hi, source],
            dst_ref=codes.at[x_hi, source],
            send_sem=code_send.at[target],
            recv_sem=code_recv.at[source],
            device_id=(dp, target * 2 + x_hi),
            device_id_type=MESH,
        )

    def half_copy(half):
        return pltpu.make_async_remote_copy(
            src_ref=codes.at[half],
            dst_ref=codes.at[half],
            send_sem=half_send,
            recv_sem=half_recv,
            device_id=(dp, z * 2 + 1 - x_hi),
            device_id_type=MESH,
        )

    for step in RING_STEPS:
        code_copy(z, (z + step) % RINGS).start()

    spread = (iota((RES, 128), 1) % RES == iota((RES, 128), 0)).astype(F32)
    tiled = dot_tn(tok, spread)
    tiled = jnp.where(iota((DEPTH, 128), 0) % 8 == iota((DEPTH, 128), 1) // RES, tiled, 0.0)
    gather = (iota((RES, DEPTH), 1) // 8 == iota((RES, DEPTH), 0)).astype(F32)
    flat = dot(gather, tiled)
    kind = iota((KINDS, 128), 0).astype(F32)
    hot = jnp.concatenate(
        [(flat[q : q + 1, :] == kind).astype(F32) for q in range(RES)], axis=1
    ).astype(BF16)
    loads[3].wait()
    feat = dot(hot, adj_v[...])
    wide_part[FEAT_BLOCK] = feat[:, :128]
    wide_part[FEAT_BLOCK + 1] = feat[:, 128:]

    loads[4].wait()
    rest = rest_v[...]
    square = jnp.sum((rest * rest).reshape(32, 8, 512), axis=0)
    square = square[:, :128] + square[:, 128:256] + square[:, 256:384] + square[:, 384:]

    loads[2].wait()
    weights = jnp.concatenate(
        [
            w_v[pl.ds(0, 153600)].reshape(1200, 128),
            jnp.concatenate(
                [w_v[pl.ds(153600, PARAMS - 153600)], jnp.zeros((ROWS * 128 - PARAMS,), F32)]
            ).reshape(8, 128),
        ],
        axis=0,
    )
    weights = weights.astype(BF16).astype(F32)
    low_lane = iota((1, 128), 1) < 64
    shifted[0:ROWS] = pltpu.roll(weights, 64, 1)
    w_out = jnp.where(low_lane, shifted[pl.ds(132, 1024), :], shifted[pl.ds(133, 1024), :])
    first = jnp.where(
        low_lane,
        shifted[pl.ds(1157, KINDS, stride=2), :],
        shifted[pl.ds(1158, KINDS, stride=2), :],
    )
    second = jnp.where(
        low_lane,
        shifted[pl.ds(1158, KINDS, stride=2), :],
        shifted[pl.ds(1159, KINDS, stride=2), :],
    )
    table = jnp.concatenate([first, second], axis=1)
    table = jnp.where(iota((KINDS, FEATURE_WIDTH), 0) < SYMBOL_KINDS, table, 0.0)
    center = jnp.mean(table, axis=1, keepdims=True)
    variance = jnp.mean((table - center) ** 2, axis=1, keepdims=True)
    inverse = lax.rsqrt(variance + norm_eps)
    unit = (table - center) * inverse
    gain = jnp.concatenate([weights[0:1], weights[1:2]], axis=1)
    shift = jnp.concatenate([weights[2:3], weights[3:4]], axis=1)
    normed = (unit * gain + shift).astype(BF16).astype(F32)
    w_rows = weights[4:132]
    pair_rows[pl.ds(0, 128, stride=2), :] = jnp.where(low_lane, w_rows, 0.0)
    pair_rows[pl.ds(1, 128, stride=2), :] = jnp.where(low_lane, pltpu.roll(w_rows, 64, 1), 0.0)
    w_pair = pair_rows[...]
    bias = jnp.where(low_lane, weights[132:133], 0.0)
    acts = (dot(normed, w_pair) + bias).astype(BF16).astype(F32)
    acts = jnp.where(iota((KINDS, 128), 0) < SYMBOL_KINDS, acts, 0.0)
    he = iota((128, 1024), 1)
    left_wide = dot(acts, (iota((128, 1024), 0) == he // 32).astype(F32))
    right_wide = dot(acts, (iota((128, 1024), 0) - 32 == he % 32).astype(F32))

    hot_own = jnp.concatenate(
        [(own[i : i + 1, :] == kind).astype(F32) for i in range(RES)], axis=0
    ).astype(BF16)

    for step in RING_STEPS:
        code_copy((z + step) % RINGS, z).wait_recv()
    half_copy(x_hi).start()
    half_copy(1 - x_hi).wait_recv()
    every = jnp.transpose(codes[...].astype(F32), (1, 0, 2, 3)).reshape(LENGTH, DEPTH)
    every = jnp.transpose(every)
    for p in range(KINDS // 2):
        pieces = []
        for v in (2 * p, 2 * p + 1):
            if v < SYMBOL_KINDS:
                hot_all = (every == float(v)).astype(F32).astype(BF16)
                pieces.append(dot(hot_own, hot_all).reshape(RES, KINDS, LENGTH))
            else:
                pieces.append(jnp.ones((RES, KINDS, LENGTH), F32))
        both = jnp.concatenate(pieces, axis=1).astype(BF16)
        for i in range(RES):
            counts[p * 48 : p * 48 + 48, i * LENGTH : (i + 1) * LENGTH] = both[i]
    loads[5].wait()
    sums = dot(counts[...], pair_v[...])
    pair_part[...] = sums.astype(BF16).reshape(PAIR_BLOCKS, PAIR_ROWS, 128)
    rows = iota((KINDS, 128), 0)
    last = jnp.where(rows < 8, sums[SYMBOL_KINDS * KINDS :], 0.0)
    wide_part[SUM_BLOCK] = jnp.concatenate([last[:8], square, last[16:]], axis=0)

    def plane_copy(part, recv, block, source, target):
        return pltpu.make_async_remote_copy(
            src_ref=part.at[block],
            dst_ref=recv.at[source],
            send_sem=plane_send.at[target],
            recv_sem=plane_recv.at[source],
            device_id=at_plane(target),
            device_id_type=MESH,
        )

    def pair_copy(block, source, target):
        return plane_copy(pair_part, pair_recv, block, source, target)

    def wide_copy(block, source, target):
        return plane_copy(wide_part, wide_recv, block, source, target)

    for p in peers:

        @pl.when(p < PAIR_BLOCKS)
        def _():
            pair_copy(p, slot, p).start()

        @pl.when((p >= PAIR_BLOCKS) & (p < PAIR_BLOCKS + ACT_BLOCK))
        def _():
            wide_copy(p - PAIR_BLOCKS, slot, p).start()

    high, low = halves(sums[: SYMBOL_KINDS * KINDS])
    w_out = w_out.astype(BF16)
    prod[...] = dot_nt(high, w_out) + dot_nt(low, w_out)
    left_sum = jnp.zeros((KINDS, 1024), F32)
    right_rows = []
    for v in range(SYMBOL_KINDS):
        block = prod[v * KINDS : (v + 1) * KINDS]
        left_sum = left_sum + right_wide[v : v + 1] * block
        right_rows.append(jnp.sum(left_wide * block, axis=0, keepdims=True))
    right_rows.append(jnp.zeros((1, 1024), F32))
    right_sum = jnp.concatenate(right_rows, axis=0)
    he_row = iota((1024, 128), 0)
    lane = iota((1024, 128), 1)
    fold_left = (he_row // 32 == lane).astype(F32)
    fold_right = (he_row % 32 == lane - 32).astype(F32)
    left_high, left_low = halves_f32(left_sum)
    right_high, right_low = halves_f32(right_sum)
    wide_part[ACT_BLOCK] = (
        dot(left_high, fold_left)
        + dot(left_low, fold_left)
        + dot(right_high, fold_right)
        + dot(right_low, fold_right)
    )

    @pl.when(slot != PAIR_BLOCKS + ACT_BLOCK)
    def _():
        wide_copy(ACT_BLOCK, slot, PAIR_BLOCKS + ACT_BLOCK).start()

    tile_u = jnp.concatenate([acts] * KINDS, axis=0)
    tile_v = jnp.concatenate(
        [jnp.broadcast_to(acts[v : v + 1], (KINDS, 128)) for v in range(KINDS)], axis=0
    )
    outer = dot_nt(fold_left, tile_u) * dot_nt(fold_right, tile_v) * (1.0 / DEPTH)
    outer_hi, outer_lo = halves(outer)
    outer_high[...] = outer_hi
    outer_low[...] = outer_lo

    def ring_copy(ring, source, target):
        return pltpu.make_async_remote_copy(
            src_ref=ring.at[source],
            dst_ref=ring.at[source],
            send_sem=ring_send.at[target],
            recv_sem=ring_recv.at[source],
            device_id=(dp, target * 2 + x_hi),
            device_id_type=MESH,
        )

    def all_copy(total, block, source, target):
        return pltpu.make_async_remote_copy(
            src_ref=total.at[block],
            dst_ref=total.at[block],
            send_sem=all_send.at[target],
            recv_sem=all_recv.at[source],
            device_id=at_plane(target),
            device_id_type=MESH,
        )

    def reduce(block, part, recv, ring, total):
        recv[slot] = part[block]
        for p in peers:
            plane_copy(part, recv, block, p, slot).wait_recv()
        ring[z] = jnp.sum(recv[...].astype(F32), axis=0).astype(ring.dtype)
        for step in RING_STEPS:
            ring_copy(ring, z, (z + step) % RINGS).start()
        for step in RING_STEPS:
            ring_copy(ring, (z + step) % RINGS, z).wait_recv()
        total[block] = jnp.sum(ring[...].astype(F32), axis=0).astype(total.dtype)
        for p in peers:
            all_copy(total, block, slot, p).start()

    @pl.when(slot < PAIR_BLOCKS)
    def _():
        reduce(slot, pair_part, pair_recv, pair_ring, pair_total)

    @pl.when((slot >= PAIR_BLOCKS) & (slot < BLOCKS))
    def _():
        reduce(slot - PAIR_BLOCKS, wide_part, wide_recv, wide_ring, wide_total)

    for p in peers:

        @pl.when(p < PAIR_BLOCKS)
        def _():
            all_copy(pair_total, p, p, slot).wait_recv()

        @pl.when((p >= PAIR_BLOCKS) & (p < BLOCKS))
        def _():
            all_copy(wide_total, p - PAIR_BLOCKS, p, slot).wait_recv()

    summed = pair_total[...].reshape(KINDS * KINDS, 128)
    w_out_grad = dot(outer_high[...], summed) + dot(outer_low[...], summed)
    act = wide_total[ACT_BLOCK] * (1.0 / DEPTH)
    act_high, act_low = halves_f32(act)
    norm_grad = dot_nt(act_high, w_pair) + dot_nt(act_low, w_pair)
    normed_t = jnp.transpose(normed)
    wide[...] = dot(normed_t, act_high) + dot(normed_t, act_low)
    w_pair_grad = wide[pl.ds(0, 128, stride=2), :] + pltpu.roll(
        wide[pl.ds(1, 128, stride=2), :], 64, 1
    )
    gained = norm_grad * gain
    feat = jnp.concatenate([wide_total[FEAT_BLOCK], wide_total[FEAT_BLOCK + 1]], axis=1)
    table_grad = feat + inverse * (
        gained
        - jnp.mean(gained, axis=1, keepdims=True)
        - unit * jnp.mean(gained * unit, axis=1, keepdims=True)
    )
    gain_grad = jnp.sum(norm_grad * unit, axis=0, keepdims=True)
    shift_grad = jnp.sum(norm_grad, axis=0, keepdims=True)
    bias_grad = jnp.sum(act, axis=0, keepdims=True)

    shifted[0:8] = jnp.zeros((8, 128), F32)
    shifted[8:1032] = pltpu.roll(w_out_grad, 64, 1)
    shifted[1032:1088] = jnp.zeros((56, 128), F32)
    shifted[1032:1033] = pltpu.roll(wide_total[SUM_BLOCK][0:1], 64, 1)
    shifted[pl.ds(1033, SYMBOL_KINDS, stride=2), :] = pltpu.roll(
        table_grad[:SYMBOL_KINDS, :128], 64, 1
    )
    shifted[pl.ds(1034, SYMBOL_KINDS, stride=2), :] = pltpu.roll(
        table_grad[:SYMBOL_KINDS, 128:], 64, 1
    )
    grad_ref[128:ROWS] = jnp.where(low_lane, shifted[3:1083], shifted[4:1084])
    grad_ref[0:4] = jnp.concatenate(
        [gain_grad[:, :128], gain_grad[:, 128:], shift_grad[:, :128], shift_grad[:, 128:]], axis=0
    )
    grad_ref[4:132] = w_pair_grad
    grad_ref[132:133] = jnp.where(low_lane, bias_grad, grad_ref[132:133])
    grad = grad_ref[...]
    squares = jnp.sum((grad * grad).reshape(ROWS // 8, 8, 128), axis=0)
    norm = jnp.sum(squares + wide_total[SUM_BLOCK][8:16])
    norm = jnp.sqrt(jnp.full((1, 512), norm, F32))
    clip_ref[...] = jnp.minimum(1.0, clip_norm / (norm + 1e-06))

    for step in RING_STEPS:
        code_copy(z, (z + step) % RINGS).wait_send()
    half_copy(x_hi).wait_send()
    for p in peers:

        @pl.when(p < PAIR_BLOCKS)
        def _():
            pair_copy(p, slot, p).wait_send()

        @pl.when((p >= PAIR_BLOCKS) & (p < BLOCKS))
        def _():
            wide_copy(p - PAIR_BLOCKS, slot, p).wait_send()

    def finish(block, ring, total):
        for step in RING_STEPS:
            ring_copy(ring, z, (z + step) % RINGS).wait_send()
        for p in peers:
            all_copy(total, block, slot, p).wait_send()

    @pl.when(slot < PAIR_BLOCKS)
    def _():
        finish(slot, pair_ring, pair_total)

    @pl.when((slot >= PAIR_BLOCKS) & (slot < BLOCKS))
    def _():
        finish(slot - PAIR_BLOCKS, wide_ring, wide_total)


def in_hbm(array):
    return pltpu.with_memory_space_constraint(array, pltpu.HBM)


def gradients(*arrays):
    return pl.pallas_call(
        kernel,
        out_shape=(
            jax.ShapeDtypeStruct((ROWS, 128), F32),
            jax.ShapeDtypeStruct((1, 512), F32),
        ),
        in_specs=[pl.BlockSpec(memory_space=pltpu.HBM)] * 6,
        out_specs=(
            pl.BlockSpec(memory_space=pltpu.VMEM),
            pl.BlockSpec(memory_space=pltpu.VMEM),
        ),
        scratch_shapes=[
            pltpu.VMEM((RES, DEPTH), jnp.int32),
            pltpu.VMEM((RES, DEPTH), jnp.int32),
            pltpu.VMEM((RES * LENGTH, 128), BF16),
            pltpu.VMEM((DEPTH * RES, FEATURE_WIDTH), BF16),
            pltpu.VMEM((PARAMS,), F32),
            pltpu.VMEM((256, 512), F32),
            pltpu.VMEM((2, RINGS, RES, DEPTH), BF16),
            pltpu.VMEM((KINDS * KINDS, RES * LENGTH), BF16),
            pltpu.VMEM((PAIR_BLOCKS, PAIR_ROWS, 128), BF16),
            pltpu.VMEM((PLANE, PAIR_ROWS, 128), BF16),
            pltpu.VMEM((RINGS, PAIR_ROWS, 128), BF16),
            pltpu.VMEM((PAIR_BLOCKS, PAIR_ROWS, 128), BF16),
            pltpu.VMEM((4, KINDS, 128), F32),
            pltpu.VMEM((PLANE, KINDS, 128), F32),
            pltpu.VMEM((RINGS, KINDS, 128), F32),
            pltpu.VMEM((4, KINDS, 128), F32),
            pltpu.VMEM((1024, KINDS * KINDS), BF16),
            pltpu.VMEM((1024, KINDS * KINDS), BF16),
            pltpu.VMEM((ROWS + 8, 128), F32),
            pltpu.VMEM((FEATURE_WIDTH, 128), F32),
            pltpu.VMEM((SYMBOL_KINDS * KINDS, 1024), F32),
            pltpu.VMEM((FEATURE_WIDTH, 128), F32),
            pltpu.SemaphoreType.DMA((6,)),
            pltpu.SemaphoreType.DMA((RINGS,)),
            pltpu.SemaphoreType.DMA((RINGS,)),
            pltpu.SemaphoreType.DMA,
            pltpu.SemaphoreType.DMA,
            pltpu.SemaphoreType.DMA((PLANE,)),
            pltpu.SemaphoreType.DMA((PLANE,)),
            pltpu.SemaphoreType.DMA((RINGS,)),
            pltpu.SemaphoreType.DMA((RINGS,)),
            pltpu.SemaphoreType.DMA((PLANE,)),
            pltpu.SemaphoreType.DMA((PLANE,)),
        ],
        compiler_params=pltpu.CompilerParams(
            collective_id=0, has_side_effects=True, vmem_limit_bytes=40 * 1024 * 1024
        ),
        cost_estimate=pl.CostEstimate(
            flops=3_000_000_000, bytes_accessed=40_000_000, transcendentals=0
        ),
    )(*[in_hbm(array) for array in arrays])


def adam_update(master, moment_one, moment_two, scaled):
    first = beta_first * moment_one + (1.0 - beta_first) * scaled
    second = beta_second * moment_two + (1.0 - beta_second) * scaled * scaled
    fix_first = 1.0 - beta_first**STEP
    fix_second = 1.0 - beta_second**STEP
    update = first * (learn_rate / fix_first) / (jnp.sqrt(second * (1.0 / fix_second)) + adam_eps)
    return (master - update, first, second)


def update_kernel(
    grad_ref,
    clip_ref,
    master_ref,
    one_ref,
    two_ref,
    rest_grad_ref,
    rest_master_ref,
    rest_one_ref,
    rest_two_ref,
    *refs,
):
    outs, held, sems = refs[:8], refs[8:16], refs[16]
    clip = clip_ref[...]
    rest_step = rest_grad_ref.shape[0] // CHUNKS
    flat_step = 1024 * 38
    copies = []

    def send(n, where):
        copy = pltpu.make_async_copy(held[n].at[where], outs[n].at[where], sems.at[len(copies)])
        copy.start()
        copies.append(copy)

    for chunk in range(CHUNKS):
        where = pl.ds(chunk * rest_step, rest_step)
        new = adam_update(
            rest_master_ref[where], rest_one_ref[where], rest_two_ref[where], rest_grad_ref[where] * clip
        )
        for n, value in enumerate(new + (new[0],)):
            held[4 + n][where] = value.astype(held[4 + n].dtype)
            send(4 + n, where)
    factor = jnp.max(clip)
    for chunk in range(CHUNKS):
        start = chunk * flat_step
        where = pl.ds(start, min(flat_step, PARAMS - start))
        new = adam_update(master_ref[where], one_ref[where], two_ref[where], grad_ref[where] * factor)
        for n, value in enumerate(new + (new[0],)):
            held[n][where] = value.astype(held[n].dtype)
            send(n, where)
    for copy in copies:
        copy.wait()


def updates(grad, clip, master, one, two, rest_grad, rest_master, rest_one, rest_two):
    flat = [jax.ShapeDtypeStruct(master.shape, dtype) for dtype in (F32, F32, F32, BF16)]
    rows = [jax.ShapeDtypeStruct(rest_master.shape, dtype) for dtype in (F32, F32, F32, BF16)]
    return pl.pallas_call(
        update_kernel,
        out_shape=tuple(flat + rows),
        in_specs=[pl.BlockSpec(memory_space=pltpu.VMEM)] * 9,
        out_specs=tuple([pl.BlockSpec(memory_space=pltpu.HBM)] * 8),
        scratch_shapes=[pltpu.VMEM(out.shape, out.dtype) for out in flat + rows]
        + [pltpu.SemaphoreType.DMA((8 * CHUNKS,))],
        compiler_params=pltpu.CompilerParams(vmem_limit_bytes=20 * 1024 * 1024),
        cost_estimate=pl.CostEstimate(
            flops=5_000_000, bytes_accessed=8_000_000, transcendentals=0
        ),
    )(grad, clip, master, one, two, rest_grad, rest_master, rest_one, rest_two)


def shards(
    symbol_codes,
    aligned_validity,
    pair_update_cotangent,
    aligned_feature_adjoint,
    local_master_weights,
    local_first_moment,
    local_second_moment,
    remaining_master_weights,
    remaining_first_moment,
    remaining_second_moment,
    remaining_gradient,
):
    gradient, clip = gradients(
        jnp.transpose(symbol_codes[0]),
        jnp.transpose(aligned_validity[0]),
        pair_update_cotangent.reshape(RES * LENGTH, 128),
        aligned_feature_adjoint.reshape(DEPTH * RES, FEATURE_WIDTH),
        local_master_weights,
        remaining_gradient,
    )
    return updates(
        gradient.reshape(-1),
        clip,
        local_master_weights,
        local_first_moment,
        local_second_moment,
        remaining_gradient,
        remaining_master_weights,
        remaining_first_moment,
        remaining_second_moment,
    )


def solution(mesh):
    return jax.shard_map(
        shards,
        mesh=mesh,
        in_specs=(
            P("dp", None, "dap"),
            P("dp", None, "dap"),
            P("dp", "dap", None, None),
            P("dp", None, "dap", None),
            P(),
            P(),
            P(),
            P(("dp", "dap"), None),
            P(("dp", "dap"), None),
            P(("dp", "dap"), None),
            P(("dp", "dap"), None),
        ),
        out_specs=(
            P(),
            P(),
            P(),
            P(),
            P(("dp", "dap"), None),
            P(("dp", "dap"), None),
            P(("dp", "dap"), None),
            P(("dp", "dap"), None),
        ),
        check_vma=False,
    )
```

time: 55.5 us -> 45.9 us (0.83)
  local copies, waits for them, and re-layouts: 5.12 us -> 0.03 us
  other arithmetic: 3.93 us -> 0 us
    convert_element_type x2 -> x0, other arithmetic: 3.93 us -> none  [the longest x1 2.44 us: shards(): new_master.astype(BF16)]
    unnamed x22 -> x14, local copies, waits for them, and re-layouts: 3.43 us -> 0.03 us
    pallas_call x1, Pallas kernels: 45.2 us -> 42.1 us  [gradients(): pl.pallas_call(kernel, out_shape=(jax.ShapeDtypeStruct((ROWS, 128), F32),...]
    pallas_call x0 -> x1, Pallas kernels: none -> 2.86 us  [updates(): pl.pallas_call(update_kernel, out_shape=tuple(flat + rows), in_specs=[pl....]
    reshape x1 -> x0, local copies, waits for them, and re-layouts: 1.18 us -> none  [shards(): jnp.pad(local_master_weights, (0, ROWS * 128 - PARAMS)).reshape(ROWS, 128)]
where the time goes in v2:
time: 45.9 us; the launch traced here: 45.8 us
  Pallas kernels  45 us (98%)
  between operations  0.76 us (2%)
    pallas_call x1, Pallas kernels, gradients(): pl.pallas_call(kernel, out_shape=(jax.ShapeDtypeStruct((ROWS, 128), F32),...  42.1 us
    pallas_call x1, Pallas kernels, updates(): pl.pallas_call(update_kernel, out_shape=tuple(flat + rows), in_specs=[pl....  2.86 us

profile of v2, /device:TPU:1, one launch (start us, length us, event | category | flops | bytes accessed | tf_op | source)
XLA Modules:
  0.0 45.8 jit_solution(16424891021852451871)
XLA Ops:
  0.6 0.0 copy-start
  0.6 0.0 copy-start.1
  0.7 0.0 copy-start.2
  0.7 0.0 copy-start.3
  0.7 0.0 copy-start.4
  0.7 0.0 copy-start.5
  0.7 0.0 copy-start.6
  0.7 42.1 %shard_map.170 = (f32[1208,128]{1,0:T(8,128)S(1)}, f32[1,512]{1,0:T(1,128)S(1)}) custom-call(s32[16,128]{1,0:T(8,128)} %bitcast.12, s32[16,128]{1,0:T(8,128)} %bitcast.13, bf16[4096,128]{1,0:T(8,128)(2,1)} %bitcast.10, bf16[2048,256]{1,0:T(8,128)(2,1)} %bitcast.11, f32[154048]{0:T(1024)} %master_ref.1, f32[256,512]{1,0:T(8,128)} %rest_grad_ref.1), custom_call_target="tpu_custom_call" | custom-call | flops 3000000000 | bytes 40000000 | tf_op jit(solution)/shard_map/pallas_call | solution.py:478
  42.9 0.0 copy-done
  42.9 0.0 copy-done.1
  42.9 0.0 copy-done.2
  42.9 0.0 copy-done.3
  42.9 0.0 copy-done.4
  42.9 0.0 copy-done.5
  42.9 0.0 copy-done.6
  42.9 2.9 %shard_map.171 = (f32[154048]{0:T(1024)}, f32[154048]{0:T(1024)}, f32[154048]{0:T(1024)}, bf16[154048]{0:T(1024)(128)(2,1)}, f32[256,512]{1,0:T(8,128)}, /*index...) custom-call(f32[154624]{0:T(1024)S(1)} %bitcast.9, f32[1,512]{1,0:T(1,128)S(1)} %get-tuple-element.11.clip_ref, ...), custom_call_target="tpu_custom_call" | custom-call | flops 5000000 | bytes 8000000 | tf_op jit(solution)/shard_map/pallas_call | solution.py:588
Async XLA Ops:
  0.6 42.2 %copy-start = (f32[154048]{0:T(1024)S(1)}, f32[154048]{0:T(1024)}, u32[]{:S(2)}) copy-start(f32[154048]{0:T(1024)} %master_ref.1) | copy-start | bytes 1848580
  0.6 42.2 %copy-start.1 = (f32[154048]{0:T(1024)S(1)}, f32[154048]{0:T(1024)}, u32[]{:S(2)}) copy-start(f32[154048]{0:T(1024)} %one_ref.1) | copy-start | bytes 1848580
  0.7 42.2 %copy-start.2 = (f32[154048]{0:T(1024)S(1)}, f32[154048]{0:T(1024)}, u32[]{:S(2)}) copy-start(f32[154048]{0:T(1024)} %two_ref.1) | copy-start | bytes 1848580
  0.7 42.2 %copy-start.3 = (f32[256,512]{1,0:T(8,128)S(1)}, f32[256,512]{1,0:T(8,128)}, u32[]{:S(2)}) copy-start(f32[256,512]{1,0:T(8,128)} %rest_grad_ref.1) | copy-start | bytes 1572868
  0.7 42.2 %copy-start.4 = (f32[256,512]{1,0:T(8,128)S(1)}, f32[256,512]{1,0:T(8,128)}, u32[]{:S(2)}) copy-start(f32[256,512]{1,0:T(8,128)} %rest_master_ref.1) | copy-start | bytes 1572868
  0.7 42.2 %copy-start.5 = (f32[256,512]{1,0:T(8,128)S(1)}, f32[256,512]{1,0:T(8,128)}, u32[]{:S(2)}) copy-start(f32[256,512]{1,0:T(8,128)} %rest_one_ref.1) | copy-start | bytes 1572868
  0.7 42.2 %copy-start.6 = (f32[256,512]{1,0:T(8,128)S(1)}, f32[256,512]{1,0:T(8,128)}, u32[]{:S(2)}) copy-start(f32[256,512]{1,0:T(8,128)} %rest_two_ref.1) | copy-start | bytes 1572868

commit v3 on v2

v3 whole, which is shorter than its diff:
```python
import jax
import jax.numpy as jnp
from jax import lax
from jax.experimental import pallas as pl
from jax.experimental.pallas import tpu as pltpu
from jax.sharding import PartitionSpec as P

FEATURE_WIDTH = 256
OUTER_LATENT = 32
SYMBOL_KINDS = 23
STEP = 10
PARAMS = 154048
ROWS = 1208
KINDS = 24
MASKED = 24.0
DEPTH = 128
RES = 16
LENGTH = 256
PLANE = 32
RINGS = 8
CROP = 16

PAIR_ROWS = 2 * KINDS
PAIR_BLOCKS = KINDS // 2
WIDE_ROWS = 32
BLOCKS = PAIR_BLOCKS + 2
CHUNKS = 4

beta_first = 0.9
beta_second = 0.999
adam_eps = 1e-06
learn_rate = 0.001
clip_norm = 0.1
norm_eps = 1e-05

MESH = pl.DeviceIdType.MESH
F32 = jnp.float32
BF16 = jnp.bfloat16


def ring_hops(step, size):
    return min(step, size - step)


PLANE_STEPS = sorted(
    (-ring_hops(dx, 4) - ring_hops(dy, 4), dx, dy, dc)
    for dx in range(4)
    for dy in range(4)
    for dc in range(2)
    if dx + dy + dc > 0
)
RING_STEPS = sorted(range(1, RINGS), key=lambda s: -ring_hops(s, RINGS))
CROP_STEPS = sorted(
    (-ring_hops(dz, RINGS) - 2 * dx, dx, dz)
    for dz in range(RINGS)
    for dx in range(2)
    if dz + dx > 0
)
NEAR = CROP // 2
CHUNK = NEAR * RES


def iota(shape, axis):
    return lax.broadcasted_iota(jnp.int32, shape, axis)


def dot(a, b):
    return jnp.dot(a, b, preferred_element_type=F32)


def dot_nt(a, b):
    return lax.dot_general(a, b, (((1,), (1,)), ((), ())), preferred_element_type=F32)


def dot_tn(a, b):
    return lax.dot_general(a, b, (((0,), (0,)), ((), ())), preferred_element_type=F32)


def halves(x):
    high = x.astype(BF16)
    return high, (x - high.astype(F32)).astype(BF16)


def halves_f32(x):
    high = x.astype(BF16).astype(F32)
    return high, x - high


def kernel(
    tok_hbm,
    valid_hbm,
    pair_hbm,
    adj_hbm,
    w_hbm,
    rest_hbm,
    grad_ref,
    clip_ref,
    tok_v,
    valid_v,
    pair_v,
    adj_v,
    w_v,
    rest_v,
    codes,
    counts,
    pair_part,
    pair_recv,
    pair_ring,
    pair_total,
    wide_part,
    wide_recv,
    wide_ring,
    wide_total,
    outer_high,
    outer_low,
    fold_left,
    fold_right,
    shifted,
    wide,
    w_out_v,
    mixed,
    pair_rows,
    normed_twice,
    local_sem,
    block_sem,
    code_send,
    code_recv,
    plane_send,
    plane_recv,
    ring_send,
    ring_recv,
    all_send,
    all_recv,
):
    dp = lax.axis_index("dp")
    dap = lax.axis_index("dap")
    z = lax.div(dap, 2)
    x_hi = lax.rem(dap, 2)
    core = lax.rem(dp, 2)
    y = lax.rem(lax.div(dp, 2), 4)
    x = x_hi * 2 + lax.div(dp, 8)

    xs = [lax.rem(x + dx, 4) for dx in range(4)]
    xs = [(lax.rem(value, 2) * 8, lax.div(value, 2)) for value in xs]
    ys = [lax.rem(y + dy, 4) * 2 for dy in range(4)]
    cores = [lax.rem(core + dc, 2) for dc in range(2)]

    def in_plane(dx, dy, dc):
        low, high = xs[dx]
        return cores[dc] * 16 + low + ys[dy] + high, (low + ys[dy] + cores[dc], z * 2 + high)

    slot = in_plane(0, 0, 0)[0]
    peers = [in_plane(*step[1:]) for step in PLANE_STEPS]
    zs = [lax.rem(z + dz, RINGS) * 2 for dz in range(RINGS)]
    mates = [zs[dz] + (1 - x_hi if dx else x_hi) for _, dx, dz in CROP_STEPS]
    order = [dap] + mates[::-1]

    loads = []
    for n, (src, dst) in enumerate(
        (
            (tok_hbm, tok_v),
            (valid_hbm, valid_v),
            (w_hbm, w_v),
            (adj_hbm, adj_v),
            (rest_hbm, rest_v),
        )
    ):
        copy = pltpu.make_async_copy(src, dst, local_sem.at[n])
        copy.start()
        loads.append(copy)

    barrier = pltpu.get_barrier_semaphore()
    greetings = [(step[0], (dp, mate)) for step, mate in zip(CROP_STEPS, mates)]
    greetings += [(step[0], peer) for step, (_, peer) in zip(PLANE_STEPS, peers)]
    for _, device in sorted(greetings, key=lambda pair: pair[0]):
        pl.semaphore_signal(barrier, inc=1, device_id=device, device_id_type=MESH)

    for n, block in enumerate(order):
        copy = pltpu.make_async_copy(
            pair_hbm.at[:, block],
            pair_v.at[n // NEAR, :, pl.ds(n % NEAR * RES, RES)],
            block_sem.at[n],
        )
        copy.start()
        loads.append(copy)

    loads[0].wait()
    loads[1].wait()
    tok = tok_v[...].astype(F32)
    own = jnp.where(valid_v[...] != 0, tok, MASKED)
    codes[dap] = own.astype(BF16)
    pl.semaphore_wait(barrier, CROP - 1 + PLANE - 1)

    def wait_all(ref, sem):
        pltpu.make_async_copy(ref, ref, sem).wait()

    for n, mate in enumerate(mates):
        pltpu.make_async_remote_copy(
            src_ref=codes.at[dap],
            dst_ref=codes.at[dap],
            send_sem=code_send,
            recv_sem=code_recv.at[0 if n >= CROP - NEAR else 1],
            device_id=(dp, mate),
            device_id_type=MESH,
        ).start()

    spread = (iota((RES, 128), 1) % RES == iota((RES, 128), 0)).astype(F32)
    tiled = dot_tn(tok, spread)
    tiled = jnp.where(iota((DEPTH, 128), 0) % 8 == iota((DEPTH, 128), 1) // RES, tiled, 0.0)
    gather = (iota((RES, DEPTH), 1) // 8 == iota((RES, DEPTH), 0)).astype(F32)
    flat = dot(gather, tiled)
    kind = iota((KINDS, 128), 0).astype(F32)
    hot = jnp.concatenate(
        [(flat[q : q + 1, :] == kind).astype(F32) for q in range(RES)], axis=1
    ).astype(BF16)
    loads[3].wait()
    feat = dot(hot, adj_v[...])
    loads[4].wait()
    rest = rest_v[...]
    square = jnp.sum((rest * rest).reshape(32, 8, 512), axis=0)
    square = square[:, :128] + square[:, 128:256] + square[:, 256:384] + square[:, 384:]
    for copy in loads[5:]:
        copy.wait()
    pair_sum = dot(
        jnp.ones((16, RES * LENGTH), BF16), pair_v[...].reshape(RES * LENGTH, 128)
    )
    wide_part[0] = jnp.concatenate([feat[:, :128], pair_sum[:8]], axis=0)
    wide_part[1] = jnp.concatenate([feat[:, 128:], square], axis=0)

    def owner_of(p):
        return ((p % 16 // 2) * 2 + p // 16, z * 2 + p % 2)

    def plane_copy(part, recv, block, target):
        return pltpu.make_async_remote_copy(
            src_ref=part.at[block],
            dst_ref=recv.at[slot],
            send_sem=plane_send.at[0 if part is pair_part else 1],
            recv_sem=plane_recv,
            device_id=owner_of(target),
            device_id_type=MESH,
        )

    def to_owners(part, recv, first):
        for block in range(part.shape[0]):

            @pl.when(slot != first + block)
            def _():
                plane_copy(part, recv, block, first + block).start()

    def owns_pair(then):
        pl.when(slot < PAIR_BLOCKS)(then)

    def owns_wide(then):
        pl.when((slot >= PAIR_BLOCKS) & (slot < BLOCKS))(then)

    to_owners(wide_part, wide_recv, PAIR_BLOCKS)

    loads[2].wait()
    weights = jnp.concatenate(
        [
            w_v[pl.ds(0, 153600)].reshape(1200, 128),
            jnp.concatenate(
                [w_v[pl.ds(153600, PARAMS - 153600)], jnp.zeros((ROWS * 128 - PARAMS,), F32)]
            ).reshape(8, 128),
        ],
        axis=0,
    )
    weights = weights.astype(BF16).astype(F32)
    low_lane = iota((1, 128), 1) < 64
    shifted[0:ROWS] = pltpu.roll(weights, 64, 1)
    w_out_v[...] = jnp.where(
        low_lane, shifted[pl.ds(132, 1024), :], shifted[pl.ds(133, 1024), :]
    )
    first = jnp.where(
        low_lane,
        shifted[pl.ds(1157, KINDS, stride=2), :],
        shifted[pl.ds(1158, KINDS, stride=2), :],
    )
    second = jnp.where(
        low_lane,
        shifted[pl.ds(1158, KINDS, stride=2), :],
        shifted[pl.ds(1159, KINDS, stride=2), :],
    )
    table = jnp.concatenate([first, second], axis=1)
    table = jnp.where(iota((KINDS, FEATURE_WIDTH), 0) < SYMBOL_KINDS, table, 0.0)
    center = jnp.mean(table, axis=1, keepdims=True)
    variance = jnp.mean((table - center) ** 2, axis=1, keepdims=True)
    inverse = lax.rsqrt(variance + norm_eps)
    unit = (table - center) * inverse
    gain = jnp.concatenate([weights[0:1], weights[1:2]], axis=1)
    shift = jnp.concatenate([weights[2:3], weights[3:4]], axis=1)
    normed = (unit * gain + shift).astype(BF16).astype(F32)
    w_rows = weights[4:132]
    pair_rows[pl.ds(0, 128, stride=2), :] = jnp.where(low_lane, w_rows, 0.0)
    pair_rows[pl.ds(1, 128, stride=2), :] = jnp.where(low_lane, pltpu.roll(w_rows, 64, 1), 0.0)
    w_pair = pair_rows[...]
    bias = jnp.where(low_lane, weights[132:133], 0.0)
    acts = (dot(normed, w_pair) + bias).astype(BF16).astype(F32)
    acts = jnp.where(iota((KINDS, 128), 0) < SYMBOL_KINDS, acts, 0.0)

    normed_twice[...] = jnp.transpose(jnp.concatenate([normed, normed], axis=0)).astype(BF16)

    he_row = iota((1024, 128), 0)
    lane = iota((1024, 128), 1)
    tile_u = jnp.concatenate([acts] * KINDS, axis=0)
    tile_v = jnp.concatenate(
        [jnp.broadcast_to(acts[v : v + 1], (KINDS, 128)) for v in range(KINDS)], axis=0
    )
    outer = dot_nt((he_row // 32 == lane).astype(F32), tile_u) * (1.0 / DEPTH)
    outer = outer * dot_nt((he_row % 32 == lane - 32).astype(F32), tile_v)
    outer_hi, outer_lo = halves(outer)
    outer_high[...] = outer_hi
    outer_low[...] = outer_lo

    def mix(weights, blocks, fold, first_row):
        blocks = jnp.concatenate(blocks, axis=1).astype(BF16)
        mixes = dot(weights.astype(BF16), blocks) * (1.0 / DEPTH)
        for h in range(OUTER_LATENT):
            mixed[pl.ds(h, KINDS, stride=32), :] = mixes[:, h * 128 : (h + 1) * 128]
        turned = jnp.concatenate([mixed[v * 32 : (v + 1) * 32] for v in range(KINDS)], axis=1)
        high, low = halves_f32(turned)
        none = jnp.zeros((OUTER_LATENT, KINDS * 128), F32)
        if first_row == 0:
            rows = [high, none, low, none]
        else:
            rows = [none, high, none, low]
        fold[...] = jnp.transpose(jnp.concatenate(rows, axis=0)).astype(BF16)

    mix(
        acts[:, OUTER_LATENT : 2 * OUTER_LATENT],
        [w_out_v[h * 32 : (h + 1) * 32] for h in range(OUTER_LATENT)],
        fold_left,
        0,
    )
    mix(
        acts[:, :OUTER_LATENT],
        [w_out_v[pl.ds(e, 32, stride=32), :] for e in range(OUTER_LATENT)],
        fold_right,
        1,
    )

    hot_own = jnp.concatenate(
        [(own[i : i + 1, :] == kind).astype(F32) for i in range(RES)], axis=0
    ).astype(BF16)

    for half in range(2):
        wait_all(codes.at[pl.ds(0, NEAR - 1 if half == 0 else CROP - NEAR)], code_recv.at[half])
        every = jnp.concatenate(
            [codes[block].astype(F32) for block in order[half * NEAR : (half + 1) * NEAR]], axis=0
        )
        every = jnp.transpose(every)
        for p in range(PAIR_BLOCKS):
            hot_all = jnp.concatenate(
                [(every == float(v)).astype(F32) for v in (2 * p, 2 * p + 1)], axis=1
            )
            both = dot(hot_own, hot_all.astype(BF16)).reshape(RES, KINDS, 2 * CHUNK)
            both = jnp.concatenate([both[:, :, :CHUNK], both[:, :, CHUNK:]], axis=1).astype(BF16)
            for i in range(RES):
                counts[
                    half, p * PAIR_ROWS : (p + 1) * PAIR_ROWS, i * CHUNK : (i + 1) * CHUNK
                ] = both[i]
        part_sums = dot(counts[half], pair_v[half].reshape(RES * CHUNK, 128))
        sums = part_sums if half == 0 else sums + part_sums
    pair_part[...] = sums.astype(BF16).reshape(PAIR_BLOCKS, PAIR_ROWS, 128)
    to_owners(pair_part, pair_recv, 0)

    def reduce(block, part, recv, ring, total, others):
        recv[slot] = part[block]
        wait_all(recv.at[pl.ds(0, PLANE - 1)], plane_recv)
        ring[z] = jnp.sum(recv[...].astype(F32), axis=0).astype(ring.dtype)
        for step in RING_STEPS:
            pltpu.make_async_remote_copy(
                src_ref=ring.at[z],
                dst_ref=ring.at[z],
                send_sem=ring_send,
                recv_sem=ring_recv,
                device_id=(dp, zs[step] + x_hi),
                device_id_type=MESH,
            ).start()
        wait_all(ring.at[pl.ds(0, RINGS - 1)], ring_recv)
        total[block] = jnp.sum(ring[...].astype(F32), axis=0).astype(total.dtype)
        for _, peer in peers:
            pltpu.make_async_remote_copy(
                src_ref=total.at[block],
                dst_ref=total.at[block],
                send_sem=all_send,
                recv_sem=all_recv.at[others],
                device_id=peer,
                device_id_type=MESH,
            ).start()

    @owns_pair
    def _():
        reduce(slot, pair_part, pair_recv, pair_ring, pair_total, 0)
        wait_all(pair_total.at[pl.ds(0, PAIR_BLOCKS - 1)], all_recv.at[0])
        wait_all(wide_total, all_recv.at[1])

    @owns_wide
    def _():
        reduce(slot - PAIR_BLOCKS, wide_part, wide_recv, wide_ring, wide_total, 1)
        wait_all(pair_total, all_recv.at[0])
        wait_all(wide_total.at[pl.ds(0, 1)], all_recv.at[1])

    @pl.when(slot >= BLOCKS)
    def _():
        wait_all(pair_total, all_recv.at[0])
        wait_all(wide_total, all_recv.at[1])

    summed = pair_total[...].reshape(KINDS * KINDS, 128)
    mixed[0 : KINDS * KINDS] = summed.astype(F32)
    by_first = jnp.concatenate([mixed[v * KINDS : (v + 1) * KINDS] for v in range(KINDS)], axis=1)
    by_second = jnp.concatenate(
        [mixed[pl.ds(u, KINDS, stride=KINDS), :] for u in range(KINDS)], axis=1
    )
    act = dot(by_first.astype(BF16), fold_left[...]) + dot(by_second.astype(BF16), fold_right[...])
    act = act + pltpu.roll(act, 64, 1)
    act = jnp.where((iota((KINDS, 128), 0) < SYMBOL_KINDS) & low_lane, act, 0.0)
    w_out_grad = dot(outer_high[...], summed) + dot(outer_low[...], summed)
    act_parts = jnp.concatenate(halves_f32(act), axis=0)
    norm_grad = dot_nt(act_parts, w_pair)
    norm_grad = norm_grad[:KINDS] + norm_grad[KINDS:]
    wide[...] = dot(normed_twice[...], act_parts.astype(BF16))
    w_pair_grad = wide[pl.ds(0, 128, stride=2), :] + pltpu.roll(
        wide[pl.ds(1, 128, stride=2), :], 64, 1
    )
    gained = norm_grad * gain
    feat = jnp.concatenate([wide_total[0][:KINDS], wide_total[1][:KINDS]], axis=1)
    table_grad = feat + inverse * (
        gained
        - jnp.mean(gained, axis=1, keepdims=True)
        - unit * jnp.mean(gained * unit, axis=1, keepdims=True)
    )
    gain_grad = jnp.sum(norm_grad * unit, axis=0, keepdims=True)
    shift_grad = jnp.sum(norm_grad, axis=0, keepdims=True)
    bias_grad = jnp.sum(act, axis=0, keepdims=True)

    shifted[0:8] = jnp.zeros((8, 128), F32)
    shifted[8:1032] = pltpu.roll(w_out_grad, 64, 1)
    shifted[1032:1088] = jnp.zeros((56, 128), F32)
    shifted[1032:1033] = pltpu.roll(wide_total[0][KINDS : KINDS + 1], 64, 1)
    shifted[pl.ds(1033, SYMBOL_KINDS, stride=2), :] = pltpu.roll(
        table_grad[:SYMBOL_KINDS, :128], 64, 1
    )
    shifted[pl.ds(1034, SYMBOL_KINDS, stride=2), :] = pltpu.roll(
        table_grad[:SYMBOL_KINDS, 128:], 64, 1
    )
    grad_ref[128:ROWS] = jnp.where(low_lane, shifted[3:1083], shifted[4:1084])
    grad_ref[0:4] = jnp.concatenate(
        [gain_grad[:, :128], gain_grad[:, 128:], shift_grad[:, :128], shift_grad[:, 128:]], axis=0
    )
    grad_ref[4:132] = w_pair_grad
    grad_ref[132:133] = jnp.where(low_lane, bias_grad, grad_ref[132:133])
    grad = grad_ref[...]
    squares = jnp.sum((grad * grad).reshape(ROWS // 8, 8, 128), axis=0)
    norm = jnp.sum(squares + wide_total[1][KINDS:])
    norm = jnp.sqrt(jnp.full((1, 512), norm, F32))
    clip_ref[...] = jnp.minimum(1.0, clip_norm / (norm + 1e-06))

    wait_all(codes.at[pl.ds(0, CROP - 1)], code_send)

    def finish(recv, ring, pairs, wides):
        wait_all(pair_part.at[pl.ds(0, pairs)], plane_send.at[0])
        wait_all(wide_part.at[pl.ds(0, wides)], plane_send.at[1])
        if recv is not None:
            wait_all(ring.at[pl.ds(0, RINGS - 1)], ring_send)
            wait_all(recv.at[pl.ds(0, PLANE - 1)], all_send)

    @owns_pair
    def _():
        finish(pair_recv, pair_ring, PAIR_BLOCKS - 1, 2)

    @owns_wide
    def _():
        finish(wide_recv, wide_ring, PAIR_BLOCKS, 1)

    @pl.when(slot >= BLOCKS)
    def _():
        finish(None, None, PAIR_BLOCKS, 2)


def in_hbm(array):
    return pltpu.with_memory_space_constraint(array, pltpu.HBM)


def gradients(*arrays):
    return pl.pallas_call(
        kernel,
        out_shape=(
            jax.ShapeDtypeStruct((ROWS, 128), F32),
            jax.ShapeDtypeStruct((1, 512), F32),
        ),
        in_specs=[pl.BlockSpec(memory_space=pltpu.HBM)] * 6,
        out_specs=(
            pl.BlockSpec(memory_space=pltpu.VMEM),
            pl.BlockSpec(memory_space=pltpu.VMEM),
        ),
        scratch_shapes=[
            pltpu.VMEM((RES, DEPTH), jnp.int32),
            pltpu.VMEM((RES, DEPTH), jnp.int32),
            pltpu.VMEM((2, RES, CHUNK, 128), BF16),
            pltpu.VMEM((DEPTH * RES, FEATURE_WIDTH), BF16),
            pltpu.VMEM((PARAMS,), F32),
            pltpu.VMEM((256, 512), F32),
            pltpu.VMEM((CROP, RES, DEPTH), BF16),
            pltpu.VMEM((2, KINDS * KINDS, RES * CHUNK), BF16),
            pltpu.VMEM((PAIR_BLOCKS, PAIR_ROWS, 128), BF16),
            pltpu.VMEM((PLANE, PAIR_ROWS, 128), BF16),
            pltpu.VMEM((RINGS, PAIR_ROWS, 128), BF16),
            pltpu.VMEM((PAIR_BLOCKS, PAIR_ROWS, 128), BF16),
            pltpu.VMEM((2, WIDE_ROWS, 128), F32),
            pltpu.VMEM((PLANE, WIDE_ROWS, 128), F32),
            pltpu.VMEM((RINGS, WIDE_ROWS, 128), F32),
            pltpu.VMEM((2, WIDE_ROWS, 128), F32),
            pltpu.VMEM((1024, KINDS * KINDS), BF16),
            pltpu.VMEM((1024, KINDS * KINDS), BF16),
            pltpu.VMEM((KINDS * 128, 128), BF16),
            pltpu.VMEM((KINDS * 128, 128), BF16),
            pltpu.VMEM((ROWS + 8, 128), F32),
            pltpu.VMEM((FEATURE_WIDTH, 128), F32),
            pltpu.VMEM((1024, 128), F32),
            pltpu.VMEM((KINDS * 32, 128), F32),
            pltpu.VMEM((FEATURE_WIDTH, 128), F32),
            pltpu.VMEM((FEATURE_WIDTH, 2 * KINDS), BF16),
            pltpu.SemaphoreType.DMA((5,)),
            pltpu.SemaphoreType.DMA((CROP,)),
            pltpu.SemaphoreType.DMA,
            pltpu.SemaphoreType.DMA((2,)),
            pltpu.SemaphoreType.DMA((2,)),
            pltpu.SemaphoreType.DMA,
            pltpu.SemaphoreType.DMA,
            pltpu.SemaphoreType.DMA,
            pltpu.SemaphoreType.DMA,
            pltpu.SemaphoreType.DMA((2,)),
        ],
        compiler_params=pltpu.CompilerParams(
            collective_id=0, has_side_effects=True, vmem_limit_bytes=40 * 1024 * 1024
        ),
        cost_estimate=pl.CostEstimate(
            flops=3_000_000_000, bytes_accessed=40_000_000, transcendentals=0
        ),
    )(*[in_hbm(array) for array in arrays])


def adam_update(master, moment_one, moment_two, scaled):
    first = beta_first * moment_one + (1.0 - beta_first) * scaled
    second = beta_second * moment_two + (1.0 - beta_second) * scaled * scaled
    fix_first = 1.0 - beta_first**STEP
    fix_second = 1.0 - beta_second**STEP
    update = first * (learn_rate / fix_first) / (jnp.sqrt(second * (1.0 / fix_second)) + adam_eps)
    return (master - update, first, second)


def update_kernel(
    grad_ref,
    clip_ref,
    master_ref,
    one_ref,
    two_ref,
    rest_grad_ref,
    rest_master_ref,
    rest_one_ref,
    rest_two_ref,
    *refs,
):
    outs, held, sems = refs[:8], refs[8:16], refs[16]
    clip = clip_ref[...]
    rest_step = rest_grad_ref.shape[0] // CHUNKS
    flat_step = 1024 * 38
    copies = []

    def send(n, where):
        copy = pltpu.make_async_copy(held[n].at[where], outs[n].at[where], sems.at[len(copies)])
        copy.start()
        copies.append(copy)

    for chunk in range(CHUNKS):
        where = pl.ds(chunk * rest_step, rest_step)
        new = adam_update(
            rest_master_ref[where], rest_one_ref[where], rest_two_ref[where], rest_grad_ref[where] * clip
        )
        for n, value in enumerate(new + (new[0],)):
            held[4 + n][where] = value.astype(held[4 + n].dtype)
            send(4 + n, where)
    factor = jnp.max(clip)
    for chunk in range(CHUNKS):
        start = chunk * flat_step
        where = pl.ds(start, min(flat_step, PARAMS - start))
        new = adam_update(master_ref[where], one_ref[where], two_ref[where], grad_ref[where] * factor)
        for n, value in enumerate(new + (new[0],)):
            held[n][where] = value.astype(held[n].dtype)
            send(n, where)
    for copy in copies:
        copy.wait()


def updates(grad, clip, master, one, two, rest_grad, rest_master, rest_one, rest_two):
    flat = [jax.ShapeDtypeStruct(master.shape, dtype) for dtype in (F32, F32, F32, BF16)]
    rows = [jax.ShapeDtypeStruct(rest_master.shape, dtype) for dtype in (F32, F32, F32, BF16)]
    return pl.pallas_call(
        update_kernel,
        out_shape=tuple(flat + rows),
        in_specs=[pl.BlockSpec(memory_space=pltpu.VMEM)] * 9,
        out_specs=tuple([pl.BlockSpec(memory_space=pltpu.HBM)] * 8),
        scratch_shapes=[pltpu.VMEM(out.shape, out.dtype) for out in flat + rows]
        + [pltpu.SemaphoreType.DMA((8 * CHUNKS,))],
        compiler_params=pltpu.CompilerParams(vmem_limit_bytes=20 * 1024 * 1024),
        cost_estimate=pl.CostEstimate(
            flops=5_000_000, bytes_accessed=8_000_000, transcendentals=0
        ),
    )(grad, clip, master, one, two, rest_grad, rest_master, rest_one, rest_two)


def shards(
    symbol_codes,
    aligned_validity,
    pair_update_cotangent,
    aligned_feature_adjoint,
    local_master_weights,
    local_first_moment,
    local_second_moment,
    remaining_master_weights,
    remaining_first_moment,
    remaining_second_moment,
    remaining_gradient,
):
    gradient, clip = gradients(
        jnp.transpose(symbol_codes[0]),
        jnp.transpose(aligned_validity[0]),
        pair_update_cotangent.reshape(RES, CROP, RES, 128),
        aligned_feature_adjoint.reshape(DEPTH * RES, FEATURE_WIDTH),
        local_master_weights,
        remaining_gradient,
    )
    return updates(
        gradient.reshape(-1),
        clip,
        local_master_weights,
        local_first_moment,
        local_second_moment,
        remaining_gradient,
        remaining_master_weights,
        remaining_first_moment,
        remaining_second_moment,
    )


def solution(mesh):
    return jax.shard_map(
        shards,
        mesh=mesh,
        in_specs=(
            P("dp", None, "dap"),
            P("dp", None, "dap"),
            P("dp", "dap", None, None),
            P("dp", None, "dap", None),
            P(),
            P(),
            P(),
            P(("dp", "dap"), None),
            P(("dp", "dap"), None),
            P(("dp", "dap"), None),
            P(("dp", "dap"), None),
        ),
        out_specs=(
            P(),
            P(),
            P(),
            P(),
            P(("dp", "dap"), None),
            P(("dp", "dap"), None),
            P(("dp", "dap"), None),
            P(("dp", "dap"), None),
        ),
        check_vma=False,
    )
```

time: 45.9 us -> 42.4 us (0.924)
  Pallas kernels: 45 us -> 41.6 us
    pallas_call x1, Pallas kernels: 42.1 us -> 38.7 us  [gradients(): pl.pallas_call(kernel, out_shape=(jax.ShapeDtypeStruct((ROWS, 128), F32),...]
where the time goes in v3:
time: 42.4 us
  Pallas kernels  41.6 us (98%)
  between operations  0.76 us (2%)
    pallas_call x1, Pallas kernels, gradients(): pl.pallas_call(kernel, out_shape=(jax.ShapeDtypeStruct((ROWS, 128), F32),...  38.7 us
    pallas_call x1, Pallas kernels, updates(): pl.pallas_call(update_kernel, out_shape=tuple(flat + rows), in_specs=[pl....  2.86 us

profile of v3, /device:TPU:1, one launch (start us, length us, event | category | flops | bytes accessed | tf_op | source)
XLA Modules:
  0.0 42.4 jit_solution(16341946430112502607)
XLA Ops:
  0.6 0.0 copy-start
  0.6 0.0 copy-start.1
  0.7 0.0 copy-start.2
  0.7 0.0 copy-start.3
  0.7 0.0 copy-start.4
  0.7 0.0 copy-start.5
  0.7 0.0 copy-start.6
  0.7 38.7 %shard_map.170 = (f32[1208,128]{1,0:T(8,128)S(1)}, f32[1,512]{1,0:T(1,128)S(1)}) custom-call(s32[16,128]{1,0:T(8,128)} %bitcast.12, s32[16,128]{1,0:T(8,128)} %bitcast.13, bf16[16,16,16,128]{3,2,1,0:T(8,128)(2,1)} %bitcast.10, bf16[2048,256]{1,0:T(8,128)(2,1)} %bitcast.11, f32[154048]{0:T(1024)} %master_ref.1, f32[256,512]{1,0:T(8,128)} %rest_grad_ref.1), custom_call_target="tpu_custom_call" | custom-call | flops 3000000000 | bytes 40000000 | tf_op jit(solution)/shard_map/pallas_call | solution.py:486
  39.4 0.0 copy-done
  39.4 0.0 copy-done.1
  39.4 0.0 copy-done.2
  39.5 0.0 copy-done.3
  39.5 0.0 copy-done.4
  39.5 0.0 copy-done.5
  39.5 0.0 copy-done.6
  39.5 2.9 %shard_map.171 = (f32[154048]{0:T(1024)}, f32[154048]{0:T(1024)}, f32[154048]{0:T(1024)}, bf16[154048]{0:T(1024)(128)(2,1)}, f32[256,512]{1,0:T(8,128)}, /*index...) custom-call(f32[154624]{0:T(1024)S(1)} %bitcast.9, f32[1,512]{1,0:T(1,128)S(1)} %get-tuple-element.11.clip_ref, ...), custom_call_target="tpu_custom_call" | custom-call | flops 5000000 | bytes 8000000 | tf_op jit(solution)/shard_map/pallas_call | solution.py:599
Async XLA Ops:
  0.6 38.8 %copy-start = (f32[154048]{0:T(1024)S(1)}, f32[154048]{0:T(1024)}, u32[]{:S(2)}) copy-start(f32[154048]{0:T(1024)} %master_ref.1) | copy-start | bytes 1848580
  0.6 38.8 %copy-start.1 = (f32[154048]{0:T(1024)S(1)}, f32[154048]{0:T(1024)}, u32[]{:S(2)}) copy-start(f32[154048]{0:T(1024)} %one_ref.1) | copy-start | bytes 1848580
  0.7 38.8 %copy-start.2 = (f32[154048]{0:T(1024)S(1)}, f32[154048]{0:T(1024)}, u32[]{:S(2)}) copy-start(f32[154048]{0:T(1024)} %two_ref.1) | copy-start | bytes 1848580
  0.7 38.8 %copy-start.3 = (f32[256,512]{1,0:T(8,128)S(1)}, f32[256,512]{1,0:T(8,128)}, u32[]{:S(2)}) copy-start(f32[256,512]{1,0:T(8,128)} %rest_grad_ref.1) | copy-start | bytes 1572868
  0.7 38.8 %copy-start.4 = (f32[256,512]{1,0:T(8,128)S(1)}, f32[256,512]{1,0:T(8,128)}, u32[]{:S(2)}) copy-start(f32[256,512]{1,0:T(8,128)} %rest_master_ref.1) | copy-start | bytes 1572868
  0.7 38.8 %copy-start.5 = (f32[256,512]{1,0:T(8,128)S(1)}, f32[256,512]{1,0:T(8,128)}, u32[]{:S(2)}) copy-start(f32[256,512]{1,0:T(8,128)} %rest_one_ref.1) | copy-start | bytes 1572868
  0.7 38.8 %copy-start.6 = (f32[256,512]{1,0:T(8,128)S(1)}, f32[256,512]{1,0:T(8,128)}, u32[]{:S(2)}) copy-start(f32[256,512]{1,0:T(8,128)} %rest_two_ref.1) | copy-start | bytes 1572868

commit v4 on v3

--- a/solution.py
+++ b/solution.py
@@ -24,7 +24,7 @@
 PAIR_BLOCKS = KINDS // 2
 WIDE_ROWS = 32
 BLOCKS = PAIR_BLOCKS + 2
-CHUNKS = 4
+CHUNKS = 8
 
 beta_first = 0.9
 beta_second = 0.999
@@ -36,6 +36,7 @@
 MESH = pl.DeviceIdType.MESH
 F32 = jnp.float32
 BF16 = jnp.bfloat16
+F8 = jnp.float8_e4m3fn
 
 
 def ring_hops(step, size):
@@ -56,8 +57,8 @@
     for dx in range(2)
     if dz + dx > 0
 )
-NEAR = CROP // 2
-CHUNK = NEAR * RES
+FIRST = 10
+STAGES = ((0, 8), (8, 12), (12, 16))
 
 
 def iota(shape, axis):
@@ -74,11 +75,6 @@
 
 def dot_tn(a, b):
     return lax.dot_general(a, b, (((0,), (0,)), ((), ())), preferred_element_type=F32)
-
-
-def halves(x):
-    high = x.astype(BF16)
-    return high, (x - high.astype(F32)).astype(BF16)
 
 
 def halves_f32(x):
@@ -97,12 +93,16 @@
     clip_ref,
     tok_v,
     valid_v,
-    pair_v,
+    pair_near,
+    pair_middle,
+    pair_far,
     adj_v,
     w_v,
     rest_v,
     codes,
-    counts,
+    counts_near,
+    counts_middle,
+    counts_far,
     pair_part,
     pair_recv,
     pair_ring,
@@ -111,15 +111,14 @@
     wide_recv,
     wide_ring,
     wide_total,
-    outer_high,
-    outer_low,
-    fold_left,
-    fold_right,
+    outer_v,
+    fold,
     shifted,
     wide,
     w_out_v,
     mixed,
     pair_rows,
+    pair_turned,
     normed_twice,
     local_sem,
     block_sem,
@@ -155,6 +154,14 @@
     mates = [zs[dz] + (1 - x_hi if dx else x_hi) for _, dx, dz in CROP_STEPS]
     order = [dap] + mates[::-1]
 
+    barrier = pltpu.get_barrier_semaphore()
+    greetings = [(step[0], (dp, mate)) for step, mate in zip(CROP_STEPS, mates)]
+    greetings += [(step[0], peer) for step, (_, peer) in zip(PLANE_STEPS, peers)]
+    greetings = [device for _, device in sorted(greetings, key=lambda pair: pair[0])]
+    for device in greetings[:FIRST]:
+        pl.semaphore_signal(barrier, inc=1, device_id=device, device_id_type=MESH)
+
+
     loads = []
     for n, (src, dst) in enumerate(
         (
@@ -169,20 +176,19 @@
         copy.start()
         loads.append(copy)
 
-    barrier = pltpu.get_barrier_semaphore()
-    greetings = [(step[0], (dp, mate)) for step, mate in zip(CROP_STEPS, mates)]
-    greetings += [(step[0], peer) for step, (_, peer) in zip(PLANE_STEPS, peers)]
-    for _, device in sorted(greetings, key=lambda pair: pair[0]):
+    for device in greetings[FIRST:]:
         pl.semaphore_signal(barrier, inc=1, device_id=device, device_id_type=MESH)
 
-    for n, block in enumerate(order):
-        copy = pltpu.make_async_copy(
-            pair_hbm.at[:, block],
-            pair_v.at[n // NEAR, :, pl.ds(n % NEAR * RES, RES)],
-            block_sem.at[n],
-        )
-        copy.start()
-        loads.append(copy)
+    cotangents = (pair_near, pair_middle, pair_far)
+    for stage, (start, stop) in enumerate(STAGES):
+        for n in range(start, stop):
+            copy = pltpu.make_async_copy(
+                pair_hbm.at[:, order[n]],
+                cotangents[stage].at[:, pl.ds((n - start) * RES, RES)],
+                block_sem.at[n],
+            )
+            copy.start()
+            loads.append(copy)
 
     loads[0].wait()
     loads[1].wait()
@@ -194,13 +200,13 @@
     def wait_all(ref, sem):
         pltpu.make_async_copy(ref, ref, sem).wait()
 
-    for n, mate in enumerate(mates):
+    for n in range(CROP - 1, 0, -1):
         pltpu.make_async_remote_copy(
             src_ref=codes.at[dap],
             dst_ref=codes.at[dap],
             send_sem=code_send,
-            recv_sem=code_recv.at[0 if n >= CROP - NEAR else 1],
-            device_id=(dp, mate),
+            recv_sem=code_recv.at[[start <= n < stop for start, stop in STAGES].index(True)],
+            device_id=(dp, order[n]),
             device_id_type=MESH,
         ).start()
 
@@ -221,9 +227,10 @@
     square = square[:, :128] + square[:, 128:256] + square[:, 256:384] + square[:, 384:]
     for copy in loads[5:]:
         copy.wait()
-    pair_sum = dot(
-        jnp.ones((16, RES * LENGTH), BF16), pair_v[...].reshape(RES * LENGTH, 128)
-    )
+    pair_sum = jnp.zeros((16, 128), F32)
+    for cotangent in cotangents:
+        rows = cotangent.shape[0] * cotangent.shape[1]
+        pair_sum = pair_sum + dot(jnp.ones((16, rows), BF16), cotangent[...].reshape(rows, 128))
     wide_part[0] = jnp.concatenate([feat[:, :128], pair_sum[:8]], axis=0)
     wide_part[1] = jnp.concatenate([feat[:, 128:], square], axis=0)
 
@@ -294,75 +301,80 @@
     pair_rows[pl.ds(0, 128, stride=2), :] = jnp.where(low_lane, w_rows, 0.0)
     pair_rows[pl.ds(1, 128, stride=2), :] = jnp.where(low_lane, pltpu.roll(w_rows, 64, 1), 0.0)
     w_pair = pair_rows[...]
+    pair_turned[...] = jnp.transpose(w_pair).astype(BF16)
     bias = jnp.where(low_lane, weights[132:133], 0.0)
     acts = (dot(normed, w_pair) + bias).astype(BF16).astype(F32)
     acts = jnp.where(iota((KINDS, 128), 0) < SYMBOL_KINDS, acts, 0.0)
 
     normed_twice[...] = jnp.transpose(jnp.concatenate([normed, normed], axis=0)).astype(BF16)
 
+    hot_own = jnp.concatenate(
+        [(own[i : i + 1, :] == kind).astype(F32) for i in range(RES)], axis=0
+    ).astype(F8)
+
+    sums = jnp.zeros((KINDS * KINDS, 128), F32)
+    for stage, (start, stop) in enumerate(STAGES):
+        wait_all(codes.at[pl.ds(0, stop - max(start, 1))], code_recv.at[stage])
+        every = jnp.concatenate([codes[block].astype(F32) for block in order[start:stop]], axis=0)
+        every = jnp.transpose(every)
+        size = (stop - start) * RES
+        counts = (counts_near, counts_middle, counts_far)[stage]
+        count = 256 // size
+        for first in range(0, KINDS, count):
+            hot_all = jnp.concatenate(
+                [(every == float(v)).astype(F32) for v in range(first, first + count)], axis=1
+            )
+            all_pairs = dot(hot_own, hot_all.astype(F8))
+            for p in range(first // 2, (first + count) // 2):
+                if size == 128:
+                    both = all_pairs.reshape(RES, KINDS, 256)
+                    both = jnp.concatenate([both[:, :, :128], both[:, :, 128:]], axis=1)
+                else:
+                    start_lane = (p - first // 2) * 128
+                    both = all_pairs[:, start_lane : start_lane + 128]
+                    turned = pltpu.roll(both, 64, 1).reshape(RES // 2, 2, KINDS, 128)
+                    both = both.reshape(RES // 2, 2, KINDS, 128)
+                    both = jnp.concatenate(
+                        [
+                            jnp.where(low_lane, both[:, 0], turned[:, 1]),
+                            jnp.where(low_lane, turned[:, 0], both[:, 1]),
+                        ],
+                        axis=1,
+                    )
+                both = both.astype(BF16)
+                for i in range(both.shape[0]):
+                    counts[p * PAIR_ROWS : (p + 1) * PAIR_ROWS, i * 128 : (i + 1) * 128] = both[i]
+        sums = sums + dot(counts[...], cotangents[stage][...].reshape(RES * size, 128))
+    pair_part[...] = sums.astype(BF16).reshape(PAIR_BLOCKS, PAIR_ROWS, 128)
+    to_owners(pair_part, pair_recv, 0)
+
     he_row = iota((1024, 128), 0)
     lane = iota((1024, 128), 1)
-    tile_u = jnp.concatenate([acts] * KINDS, axis=0)
-    tile_v = jnp.concatenate(
-        [jnp.broadcast_to(acts[v : v + 1], (KINDS, 128)) for v in range(KINDS)], axis=0
-    )
-    outer = dot_nt((he_row // 32 == lane).astype(F32), tile_u) * (1.0 / DEPTH)
-    outer = outer * dot_nt((he_row % 32 == lane - 32).astype(F32), tile_v)
-    outer_hi, outer_lo = halves(outer)
-    outer_high[...] = outer_hi
-    outer_low[...] = outer_lo
-
-    def mix(weights, blocks, fold, first_row):
+    acts_t = jnp.transpose(acts).astype(BF16)
+    left_of = dot((he_row // 32 == lane).astype(F32).astype(BF16), acts_t).astype(BF16)
+    right_of = dot((he_row % 32 == lane - 32).astype(F32).astype(BF16), acts_t).astype(BF16)
+    uv = iota((KINDS, KINDS * KINDS), 1)
+    kind_row = iota((KINDS, KINDS * KINDS), 0)
+    outer = dot(left_of, (uv % KINDS == kind_row).astype(F32).astype(BF16)) * (1.0 / DEPTH)
+    outer = outer * dot(right_of, (uv // KINDS == kind_row).astype(F32).astype(BF16))
+    outer_v[...] = outer.astype(BF16)
+
+    def mix(weights, blocks):
         blocks = jnp.concatenate(blocks, axis=1).astype(BF16)
         mixes = dot(weights.astype(BF16), blocks) * (1.0 / DEPTH)
         for h in range(OUTER_LATENT):
             mixed[pl.ds(h, KINDS, stride=32), :] = mixes[:, h * 128 : (h + 1) * 128]
         turned = jnp.concatenate([mixed[v * 32 : (v + 1) * 32] for v in range(KINDS)], axis=1)
-        high, low = halves_f32(turned)
-        none = jnp.zeros((OUTER_LATENT, KINDS * 128), F32)
-        if first_row == 0:
-            rows = [high, none, low, none]
-        else:
-            rows = [none, high, none, low]
-        fold[...] = jnp.transpose(jnp.concatenate(rows, axis=0)).astype(BF16)
-
-    mix(
+        return halves_f32(turned)
+
+    mixes = mix(
         acts[:, OUTER_LATENT : 2 * OUTER_LATENT],
         [w_out_v[h * 32 : (h + 1) * 32] for h in range(OUTER_LATENT)],
-        fold_left,
-        0,
-    )
-    mix(
+    ) + mix(
         acts[:, :OUTER_LATENT],
         [w_out_v[pl.ds(e, 32, stride=32), :] for e in range(OUTER_LATENT)],
-        fold_right,
-        1,
-    )
-
-    hot_own = jnp.concatenate(
-        [(own[i : i + 1, :] == kind).astype(F32) for i in range(RES)], axis=0
-    ).astype(BF16)
-
-    for half in range(2):
-        wait_all(codes.at[pl.ds(0, NEAR - 1 if half == 0 else CROP - NEAR)], code_recv.at[half])
-        every = jnp.concatenate(
-            [codes[block].astype(F32) for block in order[half * NEAR : (half + 1) * NEAR]], axis=0
-        )
-        every = jnp.transpose(every)
-        for p in range(PAIR_BLOCKS):
-            hot_all = jnp.concatenate(
-                [(every == float(v)).astype(F32) for v in (2 * p, 2 * p + 1)], axis=1
-            )
-            both = dot(hot_own, hot_all.astype(BF16)).reshape(RES, KINDS, 2 * CHUNK)
-            both = jnp.concatenate([both[:, :, :CHUNK], both[:, :, CHUNK:]], axis=1).astype(BF16)
-            for i in range(RES):
-                counts[
-                    half, p * PAIR_ROWS : (p + 1) * PAIR_ROWS, i * CHUNK : (i + 1) * CHUNK
-                ] = both[i]
-        part_sums = dot(counts[half], pair_v[half].reshape(RES * CHUNK, 128))
-        sums = part_sums if half == 0 else sums + part_sums
-    pair_part[...] = sums.astype(BF16).reshape(PAIR_BLOCKS, PAIR_ROWS, 128)
-    to_owners(pair_part, pair_recv, 0)
+    )
+    fold[...] = jnp.transpose(jnp.concatenate(mixes, axis=0)).astype(BF16)
 
     def reduce(block, part, recv, ring, total, others):
         recv[slot] = part[block]
@@ -412,14 +424,17 @@
     by_second = jnp.concatenate(
         [mixed[pl.ds(u, KINDS, stride=KINDS), :] for u in range(KINDS)], axis=1
     )
-    act = dot(by_first.astype(BF16), fold_left[...]) + dot(by_second.astype(BF16), fold_right[...])
-    act = act + pltpu.roll(act, 64, 1)
+    act = dot(jnp.concatenate([by_first, by_second], axis=0).astype(BF16), fold[...])
+    act = jnp.where(low_lane, act[:KINDS], act[KINDS:])
+    act = act + pltpu.roll(act, 96, 1)
+    act = jnp.where(iota((1, 128), 1) < OUTER_LATENT, act, pltpu.roll(act, 96, 1))
     act = jnp.where((iota((KINDS, 128), 0) < SYMBOL_KINDS) & low_lane, act, 0.0)
-    w_out_grad = dot(outer_high[...], summed) + dot(outer_low[...], summed)
+    w_out_grad = dot(outer_v[...], summed)
     act_parts = jnp.concatenate(halves_f32(act), axis=0)
-    norm_grad = dot_nt(act_parts, w_pair)
+    act_parts = act_parts.astype(BF16)
+    norm_grad = dot(act_parts, pair_turned[...])
     norm_grad = norm_grad[:KINDS] + norm_grad[KINDS:]
-    wide[...] = dot(normed_twice[...], act_parts.astype(BF16))
+    wide[...] = dot(normed_twice[...], act_parts)
     w_pair_grad = wide[pl.ds(0, 128, stride=2), :] + pltpu.roll(
         wide[pl.ds(1, 128, stride=2), :], 64, 1
     )
@@ -450,9 +465,20 @@
     )
     grad_ref[4:132] = w_pair_grad
     grad_ref[132:133] = jnp.where(low_lane, bias_grad, grad_ref[132:133])
-    grad = grad_ref[...]
-    squares = jnp.sum((grad * grad).reshape(ROWS // 8, 8, 128), axis=0)
-    norm = jnp.sum(squares + wide_total[1][KINDS:])
+    pair_sum = wide_total[0][KINDS : KINDS + 1]
+    single = gain_grad * gain_grad + shift_grad * shift_grad
+    single = single[:, :128] + single[:, 128:] + bias_grad * bias_grad + pair_sum * pair_sum
+    by_kind = jnp.where(iota((KINDS, FEATURE_WIDTH), 0) < SYMBOL_KINDS, table_grad, 0.0)
+    by_kind = jnp.sum((by_kind * by_kind).reshape(KINDS // 8, 8, FEATURE_WIDTH), axis=0)
+    squares = (
+        jnp.sum((w_out_grad * w_out_grad).reshape(128, 8, 128), axis=0)
+        + jnp.sum((w_pair_grad * w_pair_grad).reshape(16, 8, 128), axis=0)
+        + by_kind[:, :128]
+        + by_kind[:, 128:]
+        + wide_total[1][KINDS:]
+        + jnp.where(iota((8, 128), 0) == 0, single, 0.0)
+    )
+    norm = jnp.sum(squares)
     norm = jnp.sqrt(jnp.full((1, 512), norm, F32))
     clip_ref[...] = jnp.minimum(1.0, clip_norm / (norm + 1e-06))
 
@@ -497,12 +523,16 @@
         scratch_shapes=[
             pltpu.VMEM((RES, DEPTH), jnp.int32),
             pltpu.VMEM((RES, DEPTH), jnp.int32),
-            pltpu.VMEM((2, RES, CHUNK, 128), BF16),
+            pltpu.VMEM((RES, 128, 128), BF16),
+            pltpu.VMEM((RES, 64, 128), BF16),
+            pltpu.VMEM((RES, 64, 128), BF16),
             pltpu.VMEM((DEPTH * RES, FEATURE_WIDTH), BF16),
             pltpu.VMEM((PARAMS,), F32),
             pltpu.VMEM((256, 512), F32),
             pltpu.VMEM((CROP, RES, DEPTH), BF16),
-            pltpu.VMEM((2, KINDS * KINDS, RES * CHUNK), BF16),
+            pltpu.VMEM((KINDS * KINDS, RES * 128), BF16),
+            pltpu.VMEM((KINDS * KINDS, RES * 64), BF16),
+            pltpu.VMEM((KINDS * KINDS, RES * 64), BF16),
             pltpu.VMEM((PAIR_BLOCKS, PAIR_ROWS, 128), BF16),
             pltpu.VMEM((PLANE, PAIR_ROWS, 128), BF16),
             pltpu.VMEM((RINGS, PAIR_ROWS, 128), BF16),
@@ -512,19 +542,18 @@
             pltpu.VMEM((RINGS, WIDE_ROWS, 128), F32),
             pltpu.VMEM((2, WIDE_ROWS, 128), F32),
             pltpu.VMEM((1024, KINDS * KINDS), BF16),
-            pltpu.VMEM((1024, KINDS * KINDS), BF16),
-            pltpu.VMEM((KINDS * 128, 128), BF16),
             pltpu.VMEM((KINDS * 128, 128), BF16),
             pltpu.VMEM((ROWS + 8, 128), F32),
             pltpu.VMEM((FEATURE_WIDTH, 128), F32),
             pltpu.VMEM((1024, 128), F32),
             pltpu.VMEM((KINDS * 32, 128), F32),
             pltpu.VMEM((FEATURE_WIDTH, 128), F32),
+            pltpu.VMEM((128, FEATURE_WIDTH), BF16),
             pltpu.VMEM((FEATURE_WIDTH, 2 * KINDS), BF16),
             pltpu.SemaphoreType.DMA((5,)),
             pltpu.SemaphoreType.DMA((CROP,)),
             pltpu.SemaphoreType.DMA,
-            pltpu.SemaphoreType.DMA((2,)),
+            pltpu.SemaphoreType.DMA((len(STAGES),)),
             pltpu.SemaphoreType.DMA((2,)),
             pltpu.SemaphoreType.DMA,
             pltpu.SemaphoreType.DMA,
@@ -565,7 +594,7 @@
     outs, held, sems = refs[:8], refs[8:16], refs[16]
     clip = clip_ref[...]
     rest_step = rest_grad_ref.shape[0] // CHUNKS
-    flat_step = 1024 * 38
+    flat_step = 1024 * 19
     copies = []
 
     def send(n, where):

time: 42.4 us -> 41 us (0.967)
  Pallas kernels: 41.6 us -> 40.2 us
    pallas_call x1, Pallas kernels: 38.7 us -> 37.4 us  [gradients(): pl.pallas_call(kernel, out_shape=(jax.ShapeDtypeStruct((ROWS, 128), F32),...]
where the time goes in v4:
time: 41 us
  Pallas kernels  40.2 us (98%)
  between operations  0.76 us (2%)
    pallas_call x1, Pallas kernels, gradients(): pl.pallas_call(kernel, out_shape=(jax.ShapeDtypeStruct((ROWS, 128), F32),...  37.4 us
    pallas_call x1, Pallas kernels, updates(): pl.pallas_call(update_kernel, out_shape=tuple(flat + rows), in_specs=[pl....  2.78 us

profile of v4, /device:TPU:1, one launch (start us, length us, event | category | flops | bytes accessed | tf_op | source)
XLA Modules:
  0.0 41.0 jit_solution(322839909157368684)
XLA Ops:
  0.6 0.0 copy-start
  0.6 0.0 copy-start.1
  0.7 0.0 copy-start.2
  0.7 0.0 copy-start.3
  0.7 0.0 copy-start.4
  0.7 0.0 copy-start.5
  0.7 0.0 copy-start.6
  0.7 37.4 %shard_map.170 = (f32[1208,128]{1,0:T(8,128)S(1)}, f32[1,512]{1,0:T(1,128)S(1)}) custom-call(s32[16,128]{1,0:T(8,128)} %bitcast.12, s32[16,128]{1,0:T(8,128)} %bitcast.13, bf16[16,16,16,128]{3,2,1,0:T(8,128)(2,1)} %bitcast.10, bf16[2048,256]{1,0:T(8,128)(2,1)} %bitcast.11, f32[154048]{0:T(1024)} %master_ref.1, f32[256,512]{1,0:T(8,128)} %rest_grad_ref.1), custom_call_target="tpu_custom_call" | custom-call | flops 3000000000 | bytes 40000000 | tf_op jit(solution)/shard_map/pallas_call | solution.py:512
  38.1 0.0 copy-done
  38.1 0.0 copy-done.1
  38.1 0.0 copy-done.2
  38.1 0.0 copy-done.3
  38.2 0.0 copy-done.4
  38.2 0.0 copy-done.5
  38.2 0.0 copy-done.6
  38.2 2.8 %shard_map.171 = (f32[154048]{0:T(1024)}, f32[154048]{0:T(1024)}, f32[154048]{0:T(1024)}, bf16[154048]{0:T(1024)(128)(2,1)}, f32[256,512]{1,0:T(8,128)}, /*index...) custom-call(f32[154624]{0:T(1024)S(1)} %bitcast.9, f32[1,512]{1,0:T(1,128)S(1)} %get-tuple-element.11.clip_ref, ...), custom_call_target="tpu_custom_call" | custom-call | flops 5000000 | bytes 8000000 | tf_op jit(solution)/shard_map/pallas_call | solution.py:628
Async XLA Ops:
  0.6 37.5 %copy-start = (f32[154048]{0:T(1024)S(1)}, f32[154048]{0:T(1024)}, u32[]{:S(2)}) copy-start(f32[154048]{0:T(1024)} %master_ref.1) | copy-start | bytes 1848580
  0.6 37.5 %copy-start.1 = (f32[154048]{0:T(1024)S(1)}, f32[154048]{0:T(1024)}, u32[]{:S(2)}) copy-start(f32[154048]{0:T(1024)} %one_ref.1) | copy-start | bytes 1848580
  0.7 37.5 %copy-start.2 = (f32[154048]{0:T(1024)S(1)}, f32[154048]{0:T(1024)}, u32[]{:S(2)}) copy-start(f32[154048]{0:T(1024)} %two_ref.1) | copy-start | bytes 1848580
  0.7 37.5 %copy-start.3 = (f32[256,512]{1,0:T(8,128)S(1)}, f32[256,512]{1,0:T(8,128)}, u32[]{:S(2)}) copy-start(f32[256,512]{1,0:T(8,128)} %rest_grad_ref.1) | copy-start | bytes 1572868
  0.7 37.5 %copy-start.4 = (f32[256,512]{1,0:T(8,128)S(1)}, f32[256,512]{1,0:T(8,128)}, u32[]{:S(2)}) copy-start(f32[256,512]{1,0:T(8,128)} %rest_master_ref.1) | copy-start | bytes 1572868
  0.7 37.5 %copy-start.5 = (f32[256,512]{1,0:T(8,128)S(1)}, f32[256,512]{1,0:T(8,128)}, u32[]{:S(2)}) copy-start(f32[256,512]{1,0:T(8,128)} %rest_one_ref.1) | copy-start | bytes 1572868
  0.7 37.5 %copy-start.6 = (f32[256,512]{1,0:T(8,128)S(1)}, f32[256,512]{1,0:T(8,128)}, u32[]{:S(2)}) copy-start(f32[256,512]{1,0:T(8,128)} %rest_two_ref.1) | copy-start | bytes 1572868

commit v5 on v4

--- a/solution.py
+++ b/solution.py
@@ -32,6 +32,7 @@
 learn_rate = 0.001
 clip_norm = 0.1
 norm_eps = 1e-05
+ROOT_FLOOR = 1e-36
 
 MESH = pl.DeviceIdType.MESH
 F32 = jnp.float32
@@ -57,7 +58,6 @@
     for dx in range(2)
     if dz + dx > 0
 )
-FIRST = 10
 STAGES = ((0, 8), (8, 12), (12, 16))
 
 
@@ -158,7 +158,7 @@
     greetings = [(step[0], (dp, mate)) for step, mate in zip(CROP_STEPS, mates)]
     greetings += [(step[0], peer) for step, (_, peer) in zip(PLANE_STEPS, peers)]
     greetings = [device for _, device in sorted(greetings, key=lambda pair: pair[0])]
-    for device in greetings[:FIRST]:
+    for device in greetings:
         pl.semaphore_signal(barrier, inc=1, device_id=device, device_id_type=MESH)
 
 
@@ -175,9 +175,6 @@
         copy = pltpu.make_async_copy(src, dst, local_sem.at[n])
         copy.start()
         loads.append(copy)
-
-    for device in greetings[FIRST:]:
-        pl.semaphore_signal(barrier, inc=1, device_id=device, device_id_type=MESH)
 
     cotangents = (pair_near, pair_middle, pair_far)
     for stage, (start, stop) in enumerate(STAGES):
@@ -262,52 +259,7 @@
 
     to_owners(wide_part, wide_recv, PAIR_BLOCKS)
 
-    loads[2].wait()
-    weights = jnp.concatenate(
-        [
-            w_v[pl.ds(0, 153600)].reshape(1200, 128),
-            jnp.concatenate(
-                [w_v[pl.ds(153600, PARAMS - 153600)], jnp.zeros((ROWS * 128 - PARAMS,), F32)]
-            ).reshape(8, 128),
-        ],
-        axis=0,
-    )
-    weights = weights.astype(BF16).astype(F32)
     low_lane = iota((1, 128), 1) < 64
-    shifted[0:ROWS] = pltpu.roll(weights, 64, 1)
-    w_out_v[...] = jnp.where(
-        low_lane, shifted[pl.ds(132, 1024), :], shifted[pl.ds(133, 1024), :]
-    )
-    first = jnp.where(
-        low_lane,
-        shifted[pl.ds(1157, KINDS, stride=2), :],
-        shifted[pl.ds(1158, KINDS, stride=2), :],
-    )
-    second = jnp.where(
-        low_lane,
-        shifted[pl.ds(1158, KINDS, stride=2), :],
-        shifted[pl.ds(1159, KINDS, stride=2), :],
-    )
-    table = jnp.concatenate([first, second], axis=1)
-    table = jnp.where(iota((KINDS, FEATURE_WIDTH), 0) < SYMBOL_KINDS, table, 0.0)
-    center = jnp.mean(table, axis=1, keepdims=True)
-    variance = jnp.mean((table - center) ** 2, axis=1, keepdims=True)
-    inverse = lax.rsqrt(variance + norm_eps)
-    unit = (table - center) * inverse
-    gain = jnp.concatenate([weights[0:1], weights[1:2]], axis=1)
-    shift = jnp.concatenate([weights[2:3], weights[3:4]], axis=1)
-    normed = (unit * gain + shift).astype(BF16).astype(F32)
-    w_rows = weights[4:132]
-    pair_rows[pl.ds(0, 128, stride=2), :] = jnp.where(low_lane, w_rows, 0.0)
-    pair_rows[pl.ds(1, 128, stride=2), :] = jnp.where(low_lane, pltpu.roll(w_rows, 64, 1), 0.0)
-    w_pair = pair_rows[...]
-    pair_turned[...] = jnp.transpose(w_pair).astype(BF16)
-    bias = jnp.where(low_lane, weights[132:133], 0.0)
-    acts = (dot(normed, w_pair) + bias).astype(BF16).astype(F32)
-    acts = jnp.where(iota((KINDS, 128), 0) < SYMBOL_KINDS, acts, 0.0)
-
-    normed_twice[...] = jnp.transpose(jnp.concatenate([normed, normed], axis=0)).astype(BF16)
-
     hot_own = jnp.concatenate(
         [(own[i : i + 1, :] == kind).astype(F32) for i in range(RES)], axis=0
     ).astype(F8)
@@ -348,6 +300,51 @@
     pair_part[...] = sums.astype(BF16).reshape(PAIR_BLOCKS, PAIR_ROWS, 128)
     to_owners(pair_part, pair_recv, 0)
 
+    loads[2].wait()
+    weights = jnp.concatenate(
+        [
+            w_v[pl.ds(0, 153600)].reshape(1200, 128),
+            jnp.concatenate(
+                [w_v[pl.ds(153600, PARAMS - 153600)], jnp.zeros((ROWS * 128 - PARAMS,), F32)]
+            ).reshape(8, 128),
+        ],
+        axis=0,
+    )
+    weights = weights.astype(BF16).astype(F32)
+    shifted[0:ROWS] = pltpu.roll(weights, 64, 1)
+    w_out_v[...] = jnp.where(
+        low_lane, shifted[pl.ds(132, 1024), :], shifted[pl.ds(133, 1024), :]
+    )
+    first = jnp.where(
+        low_lane,
+        shifted[pl.ds(1157, KINDS, stride=2), :],
+        shifted[pl.ds(1158, KINDS, stride=2), :],
+    )
+    second = jnp.where(
+        low_lane,
+        shifted[pl.ds(1158, KINDS, stride=2), :],
+        shifted[pl.ds(1159, KINDS, stride=2), :],
+    )
+    table = jnp.concatenate([first, second], axis=1)
+    table = jnp.where(iota((KINDS, FEATURE_WIDTH), 0) < SYMBOL_KINDS, table, 0.0)
+    center = jnp.mean(table, axis=1, keepdims=True)
+    variance = jnp.mean((table - center) ** 2, axis=1, keepdims=True)
+    inverse = lax.rsqrt(variance + norm_eps)
+    unit = (table - center) * inverse
+    gain = jnp.concatenate([weights[0:1], weights[1:2]], axis=1)
+    shift = jnp.concatenate([weights[2:3], weights[3:4]], axis=1)
+    normed = (unit * gain + shift).astype(BF16).astype(F32)
+    w_rows = weights[4:132]
+    pair_rows[pl.ds(0, 128, stride=2), :] = jnp.where(low_lane, w_rows, 0.0)
+    pair_rows[pl.ds(1, 128, stride=2), :] = jnp.where(low_lane, pltpu.roll(w_rows, 64, 1), 0.0)
+    w_pair = pair_rows[...]
+    pair_turned[...] = jnp.transpose(w_pair).astype(BF16)
+    bias = jnp.where(low_lane, weights[132:133], 0.0)
+    acts = (dot(normed, w_pair) + bias).astype(BF16).astype(F32)
+    acts = jnp.where(iota((KINDS, 128), 0) < SYMBOL_KINDS, acts, 0.0)
+
+    normed_twice[...] = jnp.transpose(jnp.concatenate([normed, normed], axis=0)).astype(BF16)
+
     he_row = iota((1024, 128), 0)
     lane = iota((1024, 128), 1)
     acts_t = jnp.transpose(acts).astype(BF16)
@@ -429,7 +426,7 @@
     act = act + pltpu.roll(act, 96, 1)
     act = jnp.where(iota((1, 128), 1) < OUTER_LATENT, act, pltpu.roll(act, 96, 1))
     act = jnp.where((iota((KINDS, 128), 0) < SYMBOL_KINDS) & low_lane, act, 0.0)
-    w_out_grad = dot(outer_v[...], summed)
+    w_out_grad = dot(outer_v[...], pltpu.roll(mixed[0 : KINDS * KINDS], 64, 1).astype(BF16))
     act_parts = jnp.concatenate(halves_f32(act), axis=0)
     act_parts = act_parts.astype(BF16)
     norm_grad = dot(act_parts, pair_turned[...])
@@ -450,7 +447,7 @@
     bias_grad = jnp.sum(act, axis=0, keepdims=True)
 
     shifted[0:8] = jnp.zeros((8, 128), F32)
-    shifted[8:1032] = pltpu.roll(w_out_grad, 64, 1)
+    shifted[8:1032] = w_out_grad
     shifted[1032:1088] = jnp.zeros((56, 128), F32)
     shifted[1032:1033] = pltpu.roll(wide_total[0][KINDS : KINDS + 1], 64, 1)
     shifted[pl.ds(1033, SYMBOL_KINDS, stride=2), :] = pltpu.roll(
@@ -575,8 +572,11 @@
     second = beta_second * moment_two + (1.0 - beta_second) * scaled * scaled
     fix_first = 1.0 - beta_first**STEP
     fix_second = 1.0 - beta_second**STEP
-    update = first * (learn_rate / fix_first) / (jnp.sqrt(second * (1.0 / fix_second)) + adam_eps)
-    return (master - update, first, second)
+    root = second * lax.rsqrt(jnp.maximum(second, ROOT_FLOOR)) * fix_second**-0.5
+    size = root + adam_eps
+    guess = pl.reciprocal(size, approx=True)
+    guess = guess * (2.0 - size * guess)
+    return (master - first * (learn_rate / fix_first) * guess, first, second)
 
 
 def update_kernel(

time: 41 us -> 40.6 us (level)
  no operation moved by 1% of the time
where the time goes in v5:
time: 40.6 us; the launch traced here: 40.5 us
  Pallas kernels  39.8 us (98%)
  between operations  0.76 us (2%)
    pallas_call x1, Pallas kernels, gradients(): pl.pallas_call(kernel, out_shape=(jax.ShapeDtypeStruct((ROWS, 128), F32),...  37.2 us
    pallas_call x1, Pallas kernels, updates(): pl.pallas_call(update_kernel, out_shape=tuple(flat + rows), in_specs=[pl....  2.59 us

profile of v5, /device:TPU:1, one launch (start us, length us, event | category | flops | bytes accessed | tf_op | source)
XLA Modules:
  0.0 40.5 jit_solution(17592711336960425204)
XLA Ops:
  0.6 0.0 copy-start
  0.6 0.0 copy-start.1
  0.7 0.0 copy-start.2
  0.7 0.0 copy-start.3
  0.7 0.0 copy-start.4
  0.7 0.0 copy-start.5
  0.7 0.0 copy-start.6
  0.7 37.2 %shard_map.170 = (f32[1208,128]{1,0:T(8,128)S(1)}, f32[1,512]{1,0:T(1,128)S(1)}) custom-call(s32[16,128]{1,0:T(8,128)} %bitcast.12, s32[16,128]{1,0:T(8,128)} %bitcast.13, bf16[16,16,16,128]{3,2,1,0:T(8,128)(2,1)} %bitcast.10, bf16[2048,256]{1,0:T(8,128)(2,1)} %bitcast.11, f32[154048]{0:T(1024)} %master_ref.1, f32[256,512]{1,0:T(8,128)} %rest_grad_ref.1), custom_call_target="tpu_custom_call" | custom-call | flops 3000000000 | bytes 40000000 | tf_op jit(solution)/shard_map/pallas_call | solution.py:509
  37.9 0.0 copy-done
  37.9 0.0 copy-done.1
  37.9 0.0 copy-done.2
  37.9 0.0 copy-done.3
  37.9 0.0 copy-done.4
  37.9 0.0 copy-done.5
  37.9 0.0 copy-done.6
  37.9 2.6 %shard_map.171 = (f32[154048]{0:T(1024)}, f32[154048]{0:T(1024)}, f32[154048]{0:T(1024)}, bf16[154048]{0:T(1024)(128)(2,1)}, f32[256,512]{1,0:T(8,128)}, /*index...) custom-call(f32[154624]{0:T(1024)S(1)} %bitcast.9, f32[1,512]{1,0:T(1,128)S(1)} %get-tuple-element.11.clip_ref, ...), custom_call_target="tpu_custom_call" | custom-call | flops 5000000 | bytes 8000000 | tf_op jit(solution)/shard_map/pallas_call | solution.py:628
Async XLA Ops:
  0.6 37.2 %copy-start = (f32[154048]{0:T(1024)S(1)}, f32[154048]{0:T(1024)}, u32[]{:S(2)}) copy-start(f32[154048]{0:T(1024)} %master_ref.1) | copy-start | bytes 1848580
  0.6 37.2 %copy-start.1 = (f32[154048]{0:T(1024)S(1)}, f32[154048]{0:T(1024)}, u32[]{:S(2)}) copy-start(f32[154048]{0:T(1024)} %one_ref.1) | copy-start | bytes 1848580
  0.7 37.2 %copy-start.2 = (f32[154048]{0:T(1024)S(1)}, f32[154048]{0:T(1024)}, u32[]{:S(2)}) copy-start(f32[154048]{0:T(1024)} %two_ref.1) | copy-start | bytes 1848580
  0.7 37.2 %copy-start.3 = (f32[256,512]{1,0:T(8,128)S(1)}, f32[256,512]{1,0:T(8,128)}, u32[]{:S(2)}) copy-start(f32[256,512]{1,0:T(8,128)} %rest_grad_ref.1) | copy-start | bytes 1572868
  0.7 37.2 %copy-start.4 = (f32[256,512]{1,0:T(8,128)S(1)}, f32[256,512]{1,0:T(8,128)}, u32[]{:S(2)}) copy-start(f32[256,512]{1,0:T(8,128)} %rest_master_ref.1) | copy-start | bytes 1572868
  0.7 37.2 %copy-start.5 = (f32[256,512]{1,0:T(8,128)S(1)}, f32[256,512]{1,0:T(8,128)}, u32[]{:S(2)}) copy-start(f32[256,512]{1,0:T(8,128)} %rest_one_ref.1) | copy-start | bytes 1572868
  0.7 37.2 %copy-start.6 = (f32[256,512]{1,0:T(8,128)S(1)}, f32[256,512]{1,0:T(8,128)}, u32[]{:S(2)}) copy-start(f32[256,512]{1,0:T(8,128)} %rest_two_ref.1) | copy-start | bytes 1572868

commit v6 on v5

--- a/solution.py
+++ b/solution.py
@@ -24,7 +24,7 @@
 PAIR_BLOCKS = KINDS // 2
 WIDE_ROWS = 32
 BLOCKS = PAIR_BLOCKS + 2
-CHUNKS = 8
+CHUNKS = 4
 
 beta_first = 0.9
 beta_second = 0.999
@@ -594,7 +594,7 @@
     outs, held, sems = refs[:8], refs[8:16], refs[16]
     clip = clip_ref[...]
     rest_step = rest_grad_ref.shape[0] // CHUNKS
-    flat_step = 1024 * 19
+    flat_step = 1024 * 38
     copies = []
 
     def send(n, where):

time: 40.6 us -> 40.6 us (level)
  no operation moved by 1% of the time
where the time goes in v6:
time: 40.6 us; the launch traced here: 40.5 us
  Pallas kernels  39.7 us (98%)
  between operations  0.76 us (2%)
    pallas_call x1, Pallas kernels, gradients(): pl.pallas_call(kernel, out_shape=(jax.ShapeDtypeStruct((ROWS, 128), F32),...  37.2 us
    pallas_call x1, Pallas kernels, updates(): pl.pallas_call(update_kernel, out_shape=tuple(flat + rows), in_specs=[pl....  2.53 us

profile of v6, /device:TPU:1, one launch (start us, length us, event | category | flops | bytes accessed | tf_op | source)
XLA Modules:
  0.0 40.5 jit_solution(15866705706917712307)
XLA Ops:
  0.6 0.0 copy-start
  0.6 0.0 copy-start.1
  0.7 0.0 copy-start.2
  0.7 0.0 copy-start.3
  0.7 0.0 copy-start.4
  0.7 0.0 copy-start.5
  0.7 0.0 copy-start.6
  0.7 37.2 %shard_map.170 = (f32[1208,128]{1,0:T(8,128)S(1)}, f32[1,512]{1,0:T(1,128)S(1)}) custom-call(s32[16,128]{1,0:T(8,128)} %bitcast.12, s32[16,128]{1,0:T(8,128)} %bitcast.13, bf16[16,16,16,128]{3,2,1,0:T(8,128)(2,1)} %bitcast.10, bf16[2048,256]{1,0:T(8,128)(2,1)} %bitcast.11, f32[154048]{0:T(1024)} %master_ref.1, f32[256,512]{1,0:T(8,128)} %rest_grad_ref.1), custom_call_target="tpu_custom_call" | custom-call | flops 3000000000 | bytes 40000000 | tf_op jit(solution)/shard_map/pallas_call | solution.py:509
  37.9 0.0 copy-done
  37.9 0.0 copy-done.1
  37.9 0.0 copy-done.2
  37.9 0.0 copy-done.3
  37.9 0.0 copy-done.4
  37.9 0.0 copy-done.5
  37.9 0.0 copy-done.6
  37.9 2.5 %shard_map.171 = (f32[154048]{0:T(1024)}, f32[154048]{0:T(1024)}, f32[154048]{0:T(1024)}, bf16[154048]{0:T(1024)(128)(2,1)}, f32[256,512]{1,0:T(8,128)}, /*index...) custom-call(f32[154624]{0:T(1024)S(1)} %bitcast.9, f32[1,512]{1,0:T(1,128)S(1)} %get-tuple-element.11.clip_ref, ...), custom_call_target="tpu_custom_call" | custom-call | flops 5000000 | bytes 8000000 | tf_op jit(solution)/shard_map/pallas_call | solution.py:628
Async XLA Ops:
  0.6 37.2 %copy-start = (f32[154048]{0:T(1024)S(1)}, f32[154048]{0:T(1024)}, u32[]{:S(2)}) copy-start(f32[154048]{0:T(1024)} %master_ref.1) | copy-start | bytes 1848580
  0.6 37.2 %copy-start.1 = (f32[154048]{0:T(1024)S(1)}, f32[154048]{0:T(1024)}, u32[]{:S(2)}) copy-start(f32[154048]{0:T(1024)} %one_ref.1) | copy-start | bytes 1848580
  0.7 37.2 %copy-start.2 = (f32[154048]{0:T(1024)S(1)}, f32[154048]{0:T(1024)}, u32[]{:S(2)}) copy-start(f32[154048]{0:T(1024)} %two_ref.1) | copy-start | bytes 1848580
  0.7 37.2 %copy-start.3 = (f32[256,512]{1,0:T(8,128)S(1)}, f32[256,512]{1,0:T(8,128)}, u32[]{:S(2)}) copy-start(f32[256,512]{1,0:T(8,128)} %rest_grad_ref.1) | copy-start | bytes 1572868
  0.7 37.2 %copy-start.4 = (f32[256,512]{1,0:T(8,128)S(1)}, f32[256,512]{1,0:T(8,128)}, u32[]{:S(2)}) copy-start(f32[256,512]{1,0:T(8,128)} %rest_master_ref.1) | copy-start | bytes 1572868
  0.7 37.2 %copy-start.5 = (f32[256,512]{1,0:T(8,128)S(1)}, f32[256,512]{1,0:T(8,128)}, u32[]{:S(2)}) copy-start(f32[256,512]{1,0:T(8,128)} %rest_one_ref.1) | copy-start | bytes 1572868
  0.7 37.2 %copy-start.6 = (f32[256,512]{1,0:T(8,128)S(1)}, f32[256,512]{1,0:T(8,128)}, u32[]{:S(2)}) copy-start(f32[256,512]{1,0:T(8,128)} %rest_two_ref.1) | copy-start | bytes 1572868
